TPU v7x, 32 devices: a whole 2x2x4 slice. The times are simulated.
32 devices in a mesh: replica: 4 (over y, x), fsdp: 8 (over z, core).
Axes of the slice: x: 2, y: 2, z: 4, core: 2. Of those that a mesh axis runs over, the one named last changes fastest.
Arguments:
- grad_parts: bfloat16 [4, 4096, 12, 1024], P('replica', 'fsdp'), may hold values from -13 to 13
- col_widths: int32 [12], replicated, may hold values from 512 to 1024, as said below
- assignment: int32 [48], replicated, may hold values from 0 to 7, as said below
- left_stat: float32 [96, 1024, 1024], P('fsdp', 'replica'), may hold values from -1 to 40
- right_stat: float32 [96, 1024, 1024], P('fsdp', 'replica'), may hold values from -1 to 40
- left_root: bfloat16 [96, 1024, 1024], P('fsdp', None, 'replica'), may hold values from -0.25 to 5
- right_root: bfloat16 [96, 1024, 1024], P('fsdp', None, 'replica'), may hold values from -0.25 to 5
Outputs:
- update: bfloat16 [4096, 12, 1024], P('fsdp', None, 'replica')
- left_new: float32 [96, 1024, 1024], P('fsdp', 'replica')
- right_new: float32 [96, 1024, 1024], P('fsdp', 'replica')
Inputs may be any that keep to these rules, and one draw needn't show every extreme that they name: `assignment`: each worker index is named by at most 12 blocks, and some worker by exactly 12. `col_widths`: exactly one column block is 512 wide, every other one 1024.
All inputs are finite; a program needn't handle non-finite values.
Results may differ from a plain program's by a relative error of at most 0.012.
Values may be sent and summed in bfloat16 or wider, within the bound.
A program may use at most 256 MiB of HBM per device.

v0:
```python
import jax
import jax.numpy as jnp
from jax import lax
from jax.sharding import PartitionSpec as P

DECAY = 0.99
SHRINKAGE = 0.1
EPSILON = 1e-06


def slot_tables(assignment, workers, slots):
    blocks = jnp.arange(assignment.shape[0], dtype=jnp.int32)
    same_worker = assignment[:, None] == assignment[None, :]
    earlier = blocks[None, :] < blocks[:, None]
    slot_rank = jnp.sum((same_worker & earlier).astype(jnp.int32), axis=1)
    slot_ids = assignment * slots + slot_rank
    wanted = jnp.arange(workers * slots, dtype=jnp.int32)
    slot_hits = (slot_ids[None, :] == wanted[:, None]).astype(jnp.int32)
    filled = jnp.sum(slot_hits, axis=1) > 0
    block_ids = jnp.sum(slot_hits * blocks[None, :], axis=1)
    return (slot_rank, filled, block_ids)


def on_device(grad_parts, col_widths, assignment, left_stat, right_stat, left_root, right_root):
    workers = lax.axis_size("fsdp")
    me_rep = lax.axis_index("replica")
    me_work = lax.axis_index("fsdp")
    slots = left_stat.shape[0]
    quarter = left_stat.shape[1]
    block_size = left_stat.shape[2]
    rows_dev = grad_parts.shape[1]
    ncols = grad_parts.shape[2]
    per_row = block_size // rows_dev
    slot_rank, filled, block_ids = slot_tables(assignment, workers, slots)
    row_block = block_ids // ncols
    col_block = block_ids % ncols
    col_index = jnp.arange(block_size, dtype=jnp.int32)
    col_mask = (col_index[None, :] < col_widths[:, None]).astype(jnp.float32)
    terms = grad_parts[0].astype(jnp.float32) * col_mask[None]
    summed = lax.psum_scatter(
        terms.astype(jnp.bfloat16), "replica", scatter_dimension=2, tiled=True
    ).astype(jnp.float32)
    by_block = jnp.transpose(summed, (1, 0, 2))
    pick_col = col_block.reshape(workers, slots).T
    send_live = (filled & (row_block == me_work // per_row)).reshape(workers, slots).T
    outgoing = (
        jnp.take(by_block, pick_col, axis=0) * send_live.astype(jnp.float32)[:, :, None, None]
    )
    incoming = lax.all_to_all(
        outgoing.astype(jnp.bfloat16), "fsdp", split_axis=1, concat_axis=1, tiled=True
    ).astype(outgoing.dtype)
    my_blocks = lax.dynamic_slice_in_dim(block_ids, me_work * slots, slots)
    my_filled = lax.dynamic_slice_in_dim(filled, me_work * slots, slots)
    my_row = my_blocks // ncols
    my_col = my_blocks % ncols
    looked_up = jnp.sum(
        jnp.where(
            my_col[:, None] == jnp.arange(ncols, dtype=jnp.int32)[None, :], col_widths[None, :], 0
        ),
        axis=1,
    )
    my_width = jnp.where(my_filled, looked_up, block_size)

    def take_rows(received, first_row):
        return lax.dynamic_slice_in_dim(received, first_row, per_row, 0)

    pieces = jax.vmap(take_rows)(incoming, my_row * per_row)
    g_cols = pieces.reshape(slots, block_size, quarter)
    g_full = lax.all_gather(g_cols.astype(jnp.bfloat16), "replica", axis=2, tiled=True).astype(
        g_cols.dtype
    )
    left_wide = lax.all_gather(left_root, "replica", axis=2, tiled=True)
    own_rows = lax.dynamic_slice_in_dim(g_full, me_rep * quarter, quarter, 1)
    left_total = DECAY * left_stat + (1.0 - DECAY) * jnp.einsum(
        "sqk,spk->sqp", own_rows, g_full, precision=lax.Precision.HIGHEST
    )
    right_total = DECAY * right_stat + (1.0 - DECAY) * jnp.einsum(
        "skq,skp->sqp", g_cols, g_full, precision=lax.Precision.HIGHEST
    )
    global_rows = me_rep * quarter + jnp.arange(quarter, dtype=jnp.int32)
    unit_rows = (col_index[None, :] == global_rows[:, None]).astype(jnp.float32)
    within_width = (global_rows[None, :] < my_width[:, None]).astype(jnp.float32)
    left_part = jnp.sum(left_total * unit_rows[None], axis=(1, 2))
    right_part = jnp.sum(jnp.sum(right_total * unit_rows[None], axis=2) * within_width, axis=1)
    g_half = g_full.astype(jnp.bfloat16)
    left_prod = jnp.einsum(
        "sik,skp->sip", left_wide, g_half, preferred_element_type=jnp.float32
    ).astype(jnp.bfloat16)
    precond = jnp.einsum("sik,skq->siq", left_prod, right_root, preferred_element_type=jnp.float32)
    precond = precond * within_width[:, None, :]
    grad_square = jnp.sum(g_full * g_full, axis=(1, 2))
    precond_part = jnp.sum(precond * precond, axis=(1, 2))
    left_trace, right_trace, precond_square = lax.psum(
        (left_part, right_part, precond_part), "replica"
    )
    left_new = (1.0 - SHRINKAGE) * left_total + (SHRINKAGE * left_trace / block_size)[
        :, None, None
    ] * unit_rows[None]
    right_scale = SHRINKAGE * right_trace / my_width.astype(jnp.float32)
    right_new = (1.0 - SHRINKAGE) * right_total + right_scale[:, None, None] * (
        unit_rows[None] * within_width[:, :, None]
    )
    graft_scale = jnp.sqrt(grad_square / (precond_square + EPSILON))
    graft_update = (precond * graft_scale[:, None, None]).astype(jnp.bfloat16)
    update_rows = graft_update.reshape(slots, per_row, rows_dev, quarter)
    spread_rows = jnp.broadcast_to(
        update_rows[:, None], (slots, workers // per_row, per_row, rows_dev, quarter)
    )
    spread_rows = spread_rows.reshape(slots, workers, rows_dev, quarter)
    dest_group = jnp.arange(workers, dtype=jnp.int32) // per_row
    return_live = my_filled[:, None] & (my_row[:, None] == dest_group[None, :])
    returning = jnp.where(return_live[:, :, None, None], spread_rows, jnp.zeros((), jnp.bfloat16))
    arrived = lax.all_to_all(returning, "fsdp", split_axis=1, concat_axis=1, tiled=True)
    owner_first = me_work // per_row * ncols
    owner_worker = lax.dynamic_slice_in_dim(assignment, owner_first, ncols)
    owner_slot = lax.dynamic_slice_in_dim(slot_rank, owner_first, ncols)
    flattened = arrived.reshape(slots * workers, rows_dev, quarter)
    picked = jnp.take(flattened, owner_slot * workers + owner_worker, axis=0)
    update = jnp.transpose(picked, (1, 0, 2))
    return (update, left_new, right_new)


def solution(mesh):
    in_specs = (
        P("replica", "fsdp", None, None),
        P(),
        P(),
        P("fsdp", "replica", None),
        P("fsdp", "replica", None),
        P("fsdp", None, "replica"),
        P("fsdp", None, "replica"),
    )
    out_specs = (P("fsdp", None, "replica"), P("fsdp", "replica", None), P("fsdp", "replica", None))
    return jax.shard_map(
        on_device, mesh=mesh, in_specs=in_specs, out_specs=out_specs, check_vma=False
    )
```

profile of v0, /device:TPU:8, one launch (start us, length us, event | category | flops | bytes accessed | tf_op | source)
XLA Modules:
  0.0 1936.8 jit_solution(10086363905171891658)
XLA Ops:
  7.2 0.0 reduce-scatter.2.cloned.1.call-start
  7.2 0.7 fusion.8
  7.9 11.2 fusion
  19.1 0.0 copy-start.1
  19.1 0.0 reduce-scatter.2.cloned.1.call-update
  19.1 0.6 copy-done.1
  19.8 0.2 convert_reduce_fusion.1
  19.9 0.0 copy-start.3
  20.0 0.1 convert_reduce_fusion
  20.1 0.4 copy-done.3
  20.5 0.1 gt.15
  20.6 0.1 rem.63
  20.6 0.1 ne.86
  20.7 0.1 div.48
  20.8 0.1 copy.38
  20.9 0.1 reshape.213
  21.1 120.1 %reduce-scatter.2.cloned.1.call-done = bf16[512,12,256]{2,0,1:T(8,128)(2,1)} async-done(((bf16[512,12,1024]{2,0,1:T(8,128)(2,1)}), bf16[512,12,256]{2,0,1:T(8,128)(2,1)}) %reduce-scatter.2.cloned.1.call-update) | async-done | bytes 3145744 | tf_op jit(solution)/shard_map/reduce_scatter | solution.py:40
  141.2 5.2 convert_bitcast_fusion
  146.4 21.2 %gather_fusion = f32[96,512,256]{2,1,0:T(8,128)} fusion(f32[12,512,256]{2,1,0:T(8,128)} %convert_bitcast_fusion, s32[1024]{0:T(1024)S(1)} %pad_clamp_fusion.1), kind=kCustom, calls=%fused_computation | custom fusion | bytes 100663680 | tf_op jit(solution)/shard_map/jit(_take)/gather | solution.py:47
  167.6 48.9 %copy.39 = f32[12,8,512,256]{2,3,0,1:T(8,128)} copy(f32[12,8,512,256]{3,2,1,0:T(8,128)} %bitcast.39) | data formatting | bytes 100663296 | tf_op jit(solution)/shard_map/jit(_take)/gather | solution.py:47
  216.5 27.8 %multiply_convert_fusion = bf16[12,8,512,256]{2,3,0,1:T(8,128)(2,1)} fusion(f32[12,8,512,256]{2,3,0,1:T(8,128)} %copy.39, f32[12,8]{0,1:T(8,128)S(1)} %convert_bitcast_fusion.2, pred[12,8]{0,1:T(8,128)(4,1)S(1)} %compare_and_fusion), kind=kLoop, calls=%fused_computation.5 | loop fusion | flops 37748736 | bytes 75497952 | tf_op jit(solution)/shard_map/convert_element_type | solution.py:50
  244.4 6.8 all-to-all-start
  251.2 0.0 all-gather.3.cloned.1.call-start
  251.2 0.1 fusion.18
  251.3 539.8 %all-to-all-done = bf16[12,8,512,256]{2,3,0,1:T(8,128)(2,1)} async-done(((bf16[12,8,512,256]{2,3,0,1:T(8,128)(2,1)}), bf16[12,8,512,256]{2,3,0,1:T(8,128)(2,1)}, u32[]{:S(2)}, u32[]{:S(2)}) %all-to-all-start) | async-done | bytes 25165856 | tf_op jit(solution)/shard_map/all_to_all | solution.py:49
  791.1 12.6 gather_fusion.2
  803.7 0.0 copy-start
  803.7 6.3 copy.54
  810.0 0.0 all-gather.3.cloned.1.call-update
  810.0 0.2 all-gather.5.cloned.1.call-start
  810.3 0.5 all-gather.5.cloned.1.call-update
  810.8 0.1 and_select_fusion
  810.9 0.0 copy-done
  810.9 0.2 select_reduce_fusion.1
  811.1 0.1 broadcast_select_fusion
  811.2 0.1 compare_and_fusion.1
  811.2 0.1 compare_convert_fusion
  811.3 0.1 fusion.7
  811.5 14.8 gather_fusion.3
  826.2 8.8 copy.46
  835.0 203.9 %all-gather.3.cloned.1.call-done = bf16[12,1024,1024]{1,2,0:T(8,128)(2,1)} async-done(((bf16[12,1024,256]{1,2,0:T(8,128)(2,1)}), bf16[12,1024,1024]{1,2,0:T(8,128)(2,1)}) %all-gather.3.cloned.1.call-update) | async-done | bytes 25165840 | tf_op jit(solution)/shard_map/all_gather | solution.py:69
  1038.9 19.6 %fusion.3 = f32[12,256,1024]{2,1,0:T(8,128)} fusion(bf16[12,1024,1024]{1,2,0:T(8,128)(2,1)} %all-gather.3.cloned.1.call-done, s32[]{:T(128)S(6)} %select_n.103), kind=kOutput, calls=%fused_computation.20 | convolution fusion | flops 6442450944 | bytes 44040196 | tf_op jit(solution)/shard_map/sqk,spk->sqp/dot_general | solution.py:74
  1058.4 30.3 %multiply_reduce_fusion.1 = (f32[12,256]{1,0:T(8,128)S(1)}, f32[12]{0:T(128)S(1)}, f32[12,256,1024]{2,1,0:T(8,128)}) fusion(f32[256,1024]{1,0:T(8,128)S(1)} %fusion.7, f32[12,256,1024]{2,1,0:T(8,128)} %param.11, f32[12,256,1024]{2,1,0:T(8,128)} %fusion.3, f32[12,256,1024]{2,1,0:T(8,128)} %param.10, bf16[12,1024,256]{2,1,0:T(8,128)(2,1)} %bitcast.44, ...), kind=kOutput, calls=%fused_computation.12 | convolution fusion | flops 6473905152 | bytes 82849840 | tf_op jit(solution)/shard_map/skq,skp->sqp/dot_general | solution.py:77
  1088.7 0.2 fusion.10
  1088.9 179.4 %all-gather.5.cloned.1.call-done = bf16[12,1024,1024]{2,1,0:T(8,128)(2,1)} async-done(((bf16[12,1024,256]{2,1,0:T(8,128)(2,1)}), bf16[12,1024,1024]{2,1,0:T(8,128)(2,1)}) %all-gather.5.cloned.1.call-update) | async-done | bytes 25165840 | tf_op jit(solution)/shard_map/all_gather | solution.py:72
  1268.3 39.2 %multiply_reduce_fusion.3 = (f32[12]{0:T(128)S(1)}, f32[12,1024,256]{2,1,0:T(8,128)}) fusion(f32[12,256]{1,0:T(8,128)S(1)} %compare_convert_fusion, bf16[12,1024,256]{2,1,0:T(8,128)(2,1)} %param.13, bf16[12,1024,1024]{1,2,0:T(8,128)(2,1)} %all-gather.3.cloned.1.call-done, bf16[12,1024,1024]{2,1,0:T(8,128)(2,1)} %all-gather.5.cloned.1.call-done), kind=kOutput, calls=%fused_computation.18 | convolution fusion | flops 32234274816 | bytes 69218352 | tf_op jit(solution)/shard_map/sik,skq->siq/dot_general | solution.py:89
  1307.6 8.9 all-reduce.1
  1316.5 15.6 multiply_reduce_fusion
  1332.1 9.0 multiply_convert_fusion.1
  1341.0 11.0 bitcast_select_fusion
  1352.0 0.0 copy-start.2
  1352.0 0.0 copy-start.4
  1352.0 7.0 all-to-all-start.1
  1359.0 0.0 copy-done.2
  1359.0 0.0 copy-done.4
  1359.0 0.1 compare_and_fusion.2
  1359.1 27.9 %multiply_add_fusion = (f32[12,256,1024]{2,1,0:T(8,128)}, f32[12,256,1024]{2,1,0:T(8,128)}) fusion(f32[12,256]{1,0:T(8,128)S(1)} %compare_convert_fusion, f32[12]{0:T(128)S(1)} %convert_divide_fusion, f32[256,1024]{1,0:T(8,128)S(1)} %fusion.7, f32[12,256,1024]{2,1,0:T(8,128)} %get-tuple-element.22, f32[12,256,1024]{2,1,0:T(8,128)} %param.11, ...), kind=kLoop, calls=%fused_computation.11 | loop fusion | flops 40894464 | bytes 76558432 | tf_op jit(solution)/shard_map/add | solution.py:100
  1387.0 511.9 %all-to-all-done.1 = bf16[12,8,512,256]{3,2,0,1:T(8,128)(2,1)} async-done(((bf16[12,8,512,256]{3,2,0,1:T(8,128)(2,1)}), bf16[12,8,512,256]{3,2,0,1:T(8,128)(2,1)}, u32[]{:S(2)}, u32[]{:S(2)}) %all-to-all-start.1) | async-done | bytes 25165856 | tf_op jit(solution)/shard_map/all_to_all | solution.py:113
  1899.0 20.4 %copy.43 = bf16[12,8,512,256]{3,2,1,0:T(8,128)(2,1)} copy(bf16[12,8,512,256]{3,2,0,1:T(8,128)(2,1)} %all-to-all-done.1) | data formatting | bytes 50331648 | tf_op jit(solution)/shard_map/all_to_all | solution.py:113
  1919.4 8.9 gather_fusion.1
  1928.3 2.0 select_bitcast_fusion
  (13 shorter events, 0.1 us)
Async XLA Ops:
  7.2 134.0 %reduce-scatter.2.cloned.1.call-start = ((), (), s32[]{:S(2)}) async-start(), calls=%async_computation.3 | async-start | bytes 15728640 | tf_op jit(solution)/shard_map/reduce_scatter | solution.py:40
  19.1 0.7 copy-start.1
  19.9 0.5 copy-start.3
  244.4 546.8 %all-to-all-start = ((bf16[12,8,512,256]{2,3,0,1:T(8,128)(2,1)}), bf16[12,8,512,256]{2,3,0,1:T(8,128)(2,1)}, u32[]{:S(2)}, u32[]{:S(2)}) async-start(bf16[12,8,512,256]{2,3,0,1:T(8,128)(2,1)} %multiply_convert_fusion), calls=%async_computation.1 | async-start | bytes 50331648 | tf_op jit(solution)/shard_map/all_to_all | solution.py:49
  251.2 787.7 %all-gather.3.cloned.1.call-start = ((), (), s32[]{:S(2)}) async-start(), calls=%async_computation.4 | async-start | bytes 31457280 | tf_op jit(solution)/shard_map/all_gather | solution.py:69
  803.7 7.2 copy-start
  810.0 458.3 %all-gather.5.cloned.1.call-start = ((), (), s32[]{:S(2)}) async-start(), calls=%async_computation.5 | async-start | bytes 31457280 | tf_op jit(solution)/shard_map/all_gather | solution.py:72
  1352.0 7.0 copy-start.2
  1352.0 7.0 copy-start.4
  1352.0 546.9 %all-to-all-start.1 = ((bf16[12,8,512,256]{3,2,0,1:T(8,128)(2,1)}), bf16[12,8,512,256]{3,2,0,1:T(8,128)(2,1)}, u32[]{:S(2)}, u32[]{:S(2)}) async-start(bf16[12,8,512,256]{3,2,0,1:T(8,128)(2,1)} %bitcast_select_fusion), calls=%async_computation.2 | async-start | bytes 50331648 | tf_op jit(solution)/shard_map/all_to_all | solution.py:113
Sparse Core Ops, SparseCore 0:
  19.3 121.8 reduce-scatter.1
  810.2 228.6 all-gather.2
  1040.7 227.5 all-gather.4
where the time goes:
time: 1940 us
  waiting for transfers between devices  1560 us (80%)
  local copies, waits for them, and re-layouts  143 us (7%)
  other arithmetic  112 us (6%)
  matrix products  89.1 us (5%)
    all_to_all x1, waiting for transfers between devices, on_device(): lax.all_to_all(outgoing.astype(jnp.bfloat16), 'fsdp', split_axis=1, conca...  540 us
    all_to_all x1, waiting for transfers between devices, on_device(): lax.all_to_all(returning, 'fsdp', split_axis=1, concat_axis=1, tiled=True)  512 us
    all_gather x1, waiting for transfers between devices, on_device(): lax.all_gather(g_cols.astype(jnp.bfloat16), 'replica', axis=2, tiled=True)  204 us
    all_gather x1, waiting for transfers between devices, on_device(): left_wide = lax.all_gather(left_root, 'replica', axis=2, tiled=True)  179 us
    reduce_scatter x1, waiting for transfers between devices, on_device(): lax.psum_scatter(terms.astype(jnp.bfloat16), 'replica', scatter_dimension...  120 us
    gather x2, local copies, waits for them, and re-layouts, on_device(): jnp.take(by_block, pick_col, axis=0)  70.1 us
    dot_general x1, matrix products, on_device(): jnp.einsum('sik,skq->siq', left_prod, right_root, preferred_element_type=...  39.2 us
  transfers between devices with their start and end apart: 5, of which 5 were waited for; matrix products, arithmetic and copies ran while one was open for 5% of the time, Pallas kernels for 0%

commit v1 on v0

v1 whole, which is shorter than its diff:
```python
import jax
import jax.numpy as jnp
from jax import lax
from jax.experimental import pallas as pl
from jax.experimental.pallas import tpu as pltpu
from jax.sharding import PartitionSpec as P

DECAY = 0.99
SHRINKAGE = 0.1
EPSILON = 1e-06
VMEM = 56 * 1024 * 1024


def slot_tables(assignment, workers, slots):
    blocks = jnp.arange(assignment.shape[0], dtype=jnp.int32)
    same_worker = assignment[:, None] == assignment[None, :]
    earlier = blocks[None, :] < blocks[:, None]
    slot_rank = jnp.sum((same_worker & earlier).astype(jnp.int32), axis=1)
    slot_ids = assignment * slots + slot_rank
    wanted = jnp.arange(workers * slots, dtype=jnp.int32)
    slot_hits = (slot_ids[None, :] == wanted[:, None]).astype(jnp.int32)
    filled = jnp.sum(slot_hits, axis=1) > 0
    block_ids = jnp.sum(slot_hits * blocks[None, :], axis=1)
    return (slot_rank, filled, block_ids)


def pick_body(row, col, live, all_ref, out_ref, sq_ref):
    s = pl.program_id(0)
    per_row, _, rows, quarter = all_ref.shape

    @pl.when(live[s] > 0)
    def _():
        block = all_ref[...].reshape(per_row * rows, quarter)
        out_ref[0] = block
        wide = block.astype(jnp.float32)
        sq_ref[0] = jnp.sum(wide * wide, axis=0, keepdims=True)

    @pl.when(live[s] == 0)
    def _():
        out_ref[...] = jnp.zeros_like(out_ref)
        sq_ref[...] = jnp.zeros_like(sq_ref)


def pick_blocks(shards, row, col, live, per_row):
    workers, ncols, rows, quarter = shards.shape
    slots = row.shape[0]
    return pl.pallas_call(
        pick_body,
        grid_spec=pltpu.PrefetchScalarGridSpec(
            num_scalar_prefetch=3,
            grid=(slots,),
            in_specs=[
                pl.BlockSpec(
                    (per_row, 1, rows, quarter), lambda s, row, col, live: (row[s], col[s], 0, 0)
                )
            ],
            out_specs=[
                pl.BlockSpec((1, per_row * rows, quarter), lambda s, *_: (s, 0, 0)),
                pl.BlockSpec((1, 1, quarter), lambda s, *_: (s, 0, 0)),
            ],
        ),
        out_shape=[
            jax.ShapeDtypeStruct((slots, per_row * rows, quarter), jnp.bfloat16),
            jax.ShapeDtypeStruct((slots, 1, quarter), jnp.float32),
        ],
        compiler_params=pltpu.CompilerParams(vmem_limit_bytes=VMEM),
        name="pick_blocks",
    )(row, col, live, shards)


def step_body(
    ints, lscale, rscale, width, g_ref, l_ref, r_ref, ls_ref, rs_ref,
    ln_ref, rn_ref, pre_ref, sq_ref,
):
    s = pl.program_id(0)
    me, count = ints[0], ints[1]
    n, _, size, quarter = g_ref.shape
    nt = (((1,), (1,)), ((), ()))
    tn = (((0,), (0,)), ((), ()))
    keep = 1.0 - SHRINKAGE
    rows = lax.broadcasted_iota(jnp.int32, (quarter, quarter), 0)
    cols = lax.broadcasted_iota(jnp.int32, (quarter, quarter), 1)
    unit = rows == cols
    first = pl.multiple_of(me * quarter, quarter)

    @pl.when(s < count)
    def _():
        gram = None
        for r in range(n):
            part = lax.dot_general(
                g_ref[r, 0, pl.ds(first, quarter), :], g_ref[r, 0], nt,
                preferred_element_type=jnp.float32,
            )
            gram = part if gram is None else gram + part
        ln_ref[0] = (keep * DECAY) * ls_ref[0] + (keep * (1.0 - DECAY)) * gram
        mine = g_ref[me, 0]
        for r in range(n):
            at = pl.ds(r * quarter, quarter)
            part = lax.dot_general(mine, g_ref[r, 0], tn, preferred_element_type=jnp.float32)
            rn_ref[0, :, at] = (keep * DECAY) * rs_ref[0, :, at] + (keep * (1.0 - DECAY)) * part
        inner = None
        for r in range(n):
            part = jnp.dot(
                g_ref[r, 0], r_ref[0, pl.ds(r * quarter, quarter), :],
                preferred_element_type=jnp.float32,
            )
            inner = part if inner is None else inner + part
        inner = inner.astype(jnp.bfloat16)
        out = None
        for r in range(n):
            part = jnp.dot(
                l_ref[r, 0], inner[r * quarter : (r + 1) * quarter],
                preferred_element_type=jnp.float32,
            )
            out = part if out is None else out + part
        column = lax.broadcasted_iota(jnp.int32, out.shape, 1) + first
        out = jnp.where(column < width[s], out, 0.0)
        sq_ref[0] = jnp.sum(out * out, axis=0, keepdims=True)
        pre_ref[0] = out.astype(jnp.bfloat16)

    @pl.when(s >= count)
    def _():
        ln_ref[0] = (keep * DECAY) * ls_ref[0]
        rn_ref[0] = (keep * DECAY) * rs_ref[0]
        sq_ref[...] = jnp.zeros_like(sq_ref)
        pre_ref[...] = jnp.zeros_like(pre_ref)

    here = pl.ds(first, quarter)
    ln_ref[0, :, here] += jnp.where(unit, lscale[s], 0.0)
    rn_ref[0, :, here] += jnp.where(unit & (rows + first < width[s]), rscale[s], 0.0)


def step_slots(ints, lscale, rscale, width, g_all, l_all, right_root, left_stat, right_stat):
    n, slots, size, quarter = g_all.shape

    def used(s, ints):
        return jnp.minimum(s, jnp.maximum(ints[1] - 1, 0))

    gathered = pl.BlockSpec((n, 1, size, quarter), lambda s, ints, *_: (0, used(s, ints), 0, 0))
    tall = pl.BlockSpec((1, size, quarter), lambda s, ints, *_: (used(s, ints), 0, 0))
    stat = pl.BlockSpec((1, quarter, size), lambda s, *_: (s, 0, 0))
    return pl.pallas_call(
        step_body,
        grid_spec=pltpu.PrefetchScalarGridSpec(
            num_scalar_prefetch=4,
            grid=(slots,),
            in_specs=[gathered, gathered, tall, stat, stat],
            out_specs=[
                stat,
                stat,
                pl.BlockSpec((1, size, quarter), lambda s, *_: (s, 0, 0)),
                pl.BlockSpec((1, 1, quarter), lambda s, *_: (s, 0, 0)),
            ],
        ),
        out_shape=[
            jax.ShapeDtypeStruct(left_stat.shape, jnp.float32),
            jax.ShapeDtypeStruct(right_stat.shape, jnp.float32),
            jax.ShapeDtypeStruct((slots, size, quarter), jnp.bfloat16),
            jax.ShapeDtypeStruct((slots, 1, quarter), jnp.float32),
        ],
        compiler_params=pltpu.CompilerParams(vmem_limit_bytes=VMEM),
        name="step_slots",
    )(ints, lscale, rscale, width, g_all, l_all, right_root, left_stat, right_stat)


def spread_body(slot, mine, scale, pre_ref, out_ref):
    b = pl.program_id(0)
    per_row, _, rows, quarter = out_ref.shape

    @pl.when(mine[b] > 0)
    def _():
        block = pre_ref[0].astype(jnp.float32) * scale[slot[b]]
        out_ref[...] = block.astype(jnp.bfloat16).reshape(out_ref.shape)

    @pl.when(mine[b] == 0)
    def _():
        out_ref[...] = jnp.zeros_like(out_ref)


def spread_blocks(precond, slot, mine, scale, workers, ncols, rows):
    slots, size, quarter = precond.shape
    per_row = size // rows
    return pl.pallas_call(
        spread_body,
        grid_spec=pltpu.PrefetchScalarGridSpec(
            num_scalar_prefetch=3,
            grid=(slot.shape[0],),
            in_specs=[pl.BlockSpec((1, size, quarter), lambda b, slot, *_: (slot[b], 0, 0))],
            out_specs=pl.BlockSpec(
                (per_row, 1, rows, quarter), lambda b, *_: (b // ncols, b % ncols, 0, 0)
            ),
        ),
        out_shape=jax.ShapeDtypeStruct((workers, ncols, rows, quarter), jnp.bfloat16),
        compiler_params=pltpu.CompilerParams(vmem_limit_bytes=VMEM),
        name="spread_blocks",
    )(slot, mine, scale, precond)


def on_device(grad_parts, col_widths, assignment, left_stat, right_stat, left_root, right_root):
    workers = lax.axis_size("fsdp")
    me_rep = lax.axis_index("replica")
    me_work = lax.axis_index("fsdp")
    slots, quarter, block_size = left_stat.shape
    rows_dev, ncols = grad_parts.shape[1:3]
    per_row = block_size // rows_dev
    slot_rank, filled, block_ids = slot_tables(assignment, workers, slots)

    summed = lax.psum_scatter(grad_parts[0], "replica", scatter_dimension=2, tiled=True)
    left_wide = lax.all_gather(left_root, "replica", axis=0)

    my_blocks = lax.dynamic_slice_in_dim(block_ids, me_work * slots, slots)
    my_filled = lax.dynamic_slice_in_dim(filled, me_work * slots, slots)
    my_count = jnp.sum(my_filled.astype(jnp.int32))
    my_row = my_blocks // ncols
    my_col = my_blocks % ncols
    looked_up = jnp.sum(
        jnp.where(
            my_col[:, None] == jnp.arange(ncols, dtype=jnp.int32)[None, :], col_widths[None, :], 0
        ),
        axis=1,
    )
    my_width = jnp.where(my_filled, looked_up, block_size)

    first = me_rep * quarter
    global_rows = first + jnp.arange(quarter, dtype=jnp.int32)
    unit = jnp.eye(quarter, dtype=jnp.float32)
    within = (global_rows[None, :] < my_width[:, None]).astype(jnp.float32)
    left_diag = jnp.sum(lax.dynamic_slice_in_dim(left_stat, first, quarter, 2) * unit, axis=2)
    right_diag = jnp.sum(lax.dynamic_slice_in_dim(right_stat, first, quarter, 2) * unit, axis=2)
    left_part = jnp.sum(left_diag, axis=1)
    right_part = jnp.sum(right_diag * within, axis=1)

    col_mask = global_rows[None, :] < col_widths[:, None]
    masked = jnp.where(col_mask[None], summed, jnp.zeros((), jnp.bfloat16))
    shards = lax.all_gather(jnp.transpose(masked, (1, 0, 2)), "fsdp", axis=0)
    g_cols, g_sq = pick_blocks(shards, my_row, my_col, my_filled.astype(jnp.int32), per_row)
    g_all = lax.all_gather(g_cols, "replica", axis=0)
    left_trace, right_trace, grad_square = lax.psum(
        (left_part, right_part, jnp.sum(g_sq, axis=(1, 2))), "replica"
    )
    left_scale = SHRINKAGE * (DECAY * left_trace + (1.0 - DECAY) * grad_square) / block_size
    right_scale = (
        SHRINKAGE
        * (DECAY * right_trace + (1.0 - DECAY) * grad_square)
        / my_width.astype(jnp.float32)
    )
    ints = jnp.stack([me_rep.astype(jnp.int32), my_count])
    left_new, right_new, precond, p_sq = step_slots(
        ints, left_scale, right_scale, my_width, g_all, left_wide, right_root, left_stat, right_stat
    )
    precond_square = lax.psum(jnp.sum(p_sq, axis=(1, 2)), "replica")
    graft_scale = jnp.sqrt(grad_square / (precond_square + EPSILON))

    mine = (assignment == me_work).astype(jnp.int32)
    outgoing = spread_blocks(
        precond, jnp.where(mine > 0, slot_rank, 0), mine, graft_scale, workers, ncols, rows_dev
    )
    arrived = lax.psum_scatter(outgoing, "fsdp", scatter_dimension=0, tiled=False)
    update = jnp.transpose(arrived, (1, 0, 2))
    return (update, left_new, right_new)


def solution(mesh):
    in_specs = (
        P("replica", "fsdp", None, None),
        P(),
        P(),
        P("fsdp", "replica", None),
        P("fsdp", "replica", None),
        P("fsdp", None, "replica"),
        P("fsdp", None, "replica"),
    )
    out_specs = (P("fsdp", None, "replica"), P("fsdp", "replica", None), P("fsdp", "replica", None))
    return jax.shard_map(
        on_device, mesh=mesh, in_specs=in_specs, out_specs=out_specs, check_vma=False
    )
```

time: 1940 us -> 1160 us (0.60)
  waiting for transfers between devices: 1560 us -> 1030 us
  local copies, waits for them, and re-layouts: 143 us -> 0.02 us
  other arithmetic: 112 us -> 16.1 us
  matrix products: 89.1 us -> 0 us
  Pallas kernels: 0 us -> 69 us
    all_to_all x2 -> x0, waiting for transfers between devices: 1050 us -> none  [the longest x1 540 us: on_device(): lax.all_to_all(outgoing.astype(jnp.bfloat16), 'fsdp', split_axis=1, conca...]
    reduce_scatter x1 -> x2, waiting for transfers between devices: 120 us -> 385 us  [the longest x1 260 us: on_device(): lax.psum_scatter(outgoing, 'fsdp', scatter_dimension=0, tiled=False)]
    all_gather x2 -> x3, waiting for transfers between devices: 383 us -> 647 us  [the longest x1 230 us: on_device(): g_all = lax.all_gather(g_cols, 'replica', axis=0)]
    gather x6 -> x0, local copies, waits for them, and re-layouts: 115 us -> none  [the longest x2 70.1 us: on_device(): jnp.take(by_block, pick_col, axis=0)]
    dot_general x3 -> x0, matrix products: 89.1 us -> none  [the longest x1 39.2 us: on_device(): jnp.einsum('sik,skq->siq', left_prod, right_root, preferred_element_type=...]
    pallas_call x0 -> x3, Pallas kernels: none -> 69 us  [the longest x1 34.9 us: step_slots(): pl.pallas_call(step_body, grid_spec=pltpu.PrefetchScalarGridSpec(num_scal...]
    convert_element_type x7 -> x1, other arithmetic: 48.9 us -> 0.02 us  [on_device(): unit = jnp.eye(quarter, dtype=jnp.float32)]
    add x3 -> x1, other arithmetic: 27.9 us -> 0.01 us  [on_device(): global_rows = first + jnp.arange(quarter, dtype=jnp.int32)]
  transfers between devices with their start and end apart: 5 -> 5, of which waited for: 5 -> 5; matrix products, arithmetic and copies ran while one was open for 5% -> 1% of each run, Pallas kernels for 0% -> 1%
where the time goes in v1:
time: 1160 us; the launch traced here: 1150 us
  waiting for transfers between devices  1030 us (89%)
  Pallas kernels  69 us (6%)
  blocking collectives  19.2 us (2%)
  other arithmetic  16.1 us (1%)
  between operations  13.8 us (1%)
    reduce_scatter x1, waiting for transfers between devices, on_device(): lax.psum_scatter(outgoing, 'fsdp', scatter_dimension=0, tiled=False)  260 us
    all_gather x1, waiting for transfers between devices, on_device(): g_all = lax.all_gather(g_cols, 'replica', axis=0)  230 us
    all_gather x1, waiting for transfers between devices, on_device(): shards = lax.all_gather(jnp.transpose(masked, (1, 0, 2)), 'fsdp', axis=0)  213 us
    all_gather x1, waiting for transfers between devices, on_device(): left_wide = lax.all_gather(left_root, 'replica', axis=0)  204 us
    reduce_scatter x1, waiting for transfers between devices, on_device(): lax.psum_scatter(grad_parts[0], 'replica', scatter_dimension=2, tiled=True)  125 us
    pallas_call x1, Pallas kernels, step_slots(): pl.pallas_call(step_body, grid_spec=pltpu.PrefetchScalarGridSpec(num_scal...  34.9 us
    pallas_call x1, Pallas kernels, spread_blocks(): pl.pallas_call(spread_body, grid_spec=pltpu.PrefetchScalarGridSpec(num_sc...  25.6 us
  transfers between devices with their start and end apart: 5, of which 5 were waited for; matrix products, arithmetic and copies ran while one was open for 1% of the time, Pallas kernels for 1%

profile of v1, /device:TPU:8, one launch (start us, length us, event | category | flops | bytes accessed | tf_op | source)
XLA Modules:
  0.0 1152.0 jit_solution(11818655482275092582)
XLA Ops:
  7.2 0.0 reduce-scatter.3.cloned.1.call-start
  7.2 0.0 copy-start.4
  7.2 0.7 reduce-scatter.3.cloned.1.call-update
  7.9 0.0 all-gather.7.cloned.1.call-start
  8.0 0.0 copy-done.4
  8.0 0.1 broadcast_compare_fusion
  8.0 125.0 %reduce-scatter.3.cloned.1.call-done = bf16[512,12,256]{2,0,1:T(8,128)(2,1)} async-done(((bf16[512,12,1024]{2,0,1:T(8,128)(2,1)}), bf16[512,12,256]{2,0,1:T(8,128)(2,1)}) %reduce-scatter.3.cloned.1.call-update) | async-done | bytes 3145744 | tf_op jit(solution)/shard_map/reduce_scatter | solution.py:208
  133.0 3.8 select_bitcast_fusion
  136.8 0.0 copy-start.3
  136.8 0.0 all-gather.7.cloned.1.call-update
  136.8 0.0 all-gather.11.cloned.1.call-start
  136.9 0.7 all-gather.11.cloned.1.call-update
  137.6 0.0 all-gather.9.cloned.1.call-start
  137.6 0.0 copy-done.3
  137.6 0.2 convert_reduce_fusion.1
  137.8 0.5 compare_select_fusion
  138.3 0.1 convert_reduce_fusion
  138.4 0.6 and_select_fusion
  139.0 0.0 copy-start.2
  139.0 0.2 select_reduce_fusion.2
  139.2 1.4 fusion.3
  140.6 0.0 copy-start.1
  140.6 213.3 %all-gather.7.cloned.1.call-done = bf16[96,512,256]{2,1,0:T(8,128)(2,1)} async-done(((bf16[12,512,256]{2,1,0:T(8,128)(2,1)}), bf16[96,512,256]{2,1,0:T(8,128)(2,1)}) %all-gather.7.cloned.1.call-update) | async-done | bytes 25165840 | tf_op jit(solution)/shard_map/all_gather | solution.py:235
  353.9 0.0 copy-done.2
  353.9 8.6 pick_blocks.1
  362.4 0.0 copy-start
  362.4 0.0 all-gather.9.cloned.1.call-update
  362.4 0.0 reduce-scatter.5.cloned.1.call-start
  362.5 1.3 pad_add_fusion.ints
  363.8 5.7 multiply_reduce_fusion
  369.5 0.2 select_reduce_fusion.1
  369.7 0.0 copy-done
  369.7 0.2 reduce_sum.97
  369.9 10.3 all-reduce
  380.2 0.0 copy-done.1
  380.2 0.5 convert_divide_fusion
  380.7 204.0 %all-gather.11.cloned.1.call-done = bf16[48,1024,256]{2,1,0:T(8,128)(2,1)} async-done(((bf16[12,1024,256]{2,1,0:T(8,128)(2,1)}), bf16[48,1024,256]{2,1,0:T(8,128)(2,1)}) %all-gather.11.cloned.1.call-update) | async-done | bytes 25165840 | tf_op jit(solution)/shard_map/all_gather | solution.py:209
  584.7 230.0 %all-gather.9.cloned.1.call-done = bf16[48,1024,256]{2,1,0:T(8,128)(2,1)} async-done(((bf16[12,1024,256]{2,1,0:T(8,128)(2,1)}), bf16[48,1024,256]{2,1,0:T(8,128)(2,1)}) %all-gather.9.cloned.1.call-update) | async-done | bytes 25165840 | tf_op jit(solution)/shard_map/all_gather | solution.py:237
  814.8 34.9 %step_slots.1 = (f32[12,256,1024]{2,1,0:T(8,128)}, f32[12,256,1024]{2,1,0:T(8,128)}, bf16[12,1024,256]{2,1,0:T(8,128)(2,1)}, f32[12,1,256]{2,1,0:T(1,128)}) custom-call(s32[2]{0:T(128)} %pad_add_fusion.ints, f32[12]{0:T(128)} %get-tuple-element.28.lscale, f32[12]{0:T(128)} %get-tuple-element.27.rscale, s32[12]{0:T(128)} %copy-done.1, ...), custom_call_target="tpu_custom_call" | custom-call | tf_op jit(solution)/shard_map/step_slots/pallas_call | solution.py:142
  849.6 0.9 reduce_sum.103
  850.5 8.9 psum.31
  859.5 0.5 fusion.2.scale
  860.0 25.6 %spread_blocks.1 = bf16[8,12,512,256]{3,2,1,0:T(8,128)(2,1)} custom-call(s32[48]{0:T(128)} %get-tuple-element.24.slot, s32[48]{0:T(128)} %get-tuple-element.25.mine, f32[12]{0:T(128)} %fusion.2.scale, bf16[12,1024,256]{2,1,0:T(8,128)(2,1)} %get-tuple-element.12.pre_ref), custom_call_target="tpu_custom_call" | custom-call | tf_op jit(solution)/shard_map/spread_blocks/pallas_call | solution.py:183
  885.6 0.0 reduce-scatter.5.cloned.1.call-update
  885.6 259.9 %reduce-scatter.5.cloned.1.call-done = bf16[1,12,512,256]{3,2,1,0:T(8,128)(2,1)} async-done(((bf16[8,12,512,256]{3,2,1,0:T(8,128)(2,1)}), bf16[1,12,512,256]{3,2,1,0:T(8,128)(2,1)}) %reduce-scatter.5.cloned.1.call-update) | async-done | bytes 3145744 | tf_op jit(solution)/shard_map/reduce_scatter | solution.py:258
  (3 shorter events, 0.0 us)
Async XLA Ops:
  7.2 125.9 %reduce-scatter.3.cloned.1.call-start = ((), (), s32[]{:S(2)}) async-start(), calls=%async_computation.2 | async-start | bytes 15728640 | tf_op jit(solution)/shard_map/reduce_scatter | solution.py:208
  7.2 0.8 copy-start.4
  7.9 346.0 %all-gather.7.cloned.1.call-start = ((), (), s32[]{:S(2)}) async-start(), calls=%async_computation.4 | async-start | bytes 28311552 | tf_op jit(solution)/shard_map/all_gather | solution.py:235
  136.8 0.8 copy-start.3
  136.8 447.9 %all-gather.11.cloned.1.call-start = ((), (), s32[]{:S(2)}) async-start(), calls=%async_computation.6 | async-start | bytes 31457280 | tf_op jit(solution)/shard_map/all_gather | solution.py:209
  137.6 677.2 %all-gather.9.cloned.1.call-start = ((), (), s32[]{:S(2)}) async-start(), calls=%async_computation.5 | async-start | bytes 31457280 | tf_op jit(solution)/shard_map/all_gather | solution.py:237
  139.0 214.8 %copy-start.2 = (s32[12]{0:T(128)}, s32[12]{0:T(128)S(1)}, u32[]{:S(2)}) copy-start(s32[12]{0:T(128)S(1)} %get-tuple-element.30.col) | copy-start | bytes 148
  140.6 239.6 %copy-start.1 = (s32[12]{0:T(128)}, s32[12]{0:T(128)S(1)}, u32[]{:S(2)}) copy-start(s32[12]{0:T(128)S(1)} %get-tuple-element.29.width) | copy-start | bytes 148
  362.4 7.3 copy-start
  362.4 783.0 %reduce-scatter.5.cloned.1.call-start = ((), (), s32[]{:S(2)}) async-start(), calls=%async_computation.3 | async-start | bytes 28311552 | tf_op jit(solution)/shard_map/reduce_scatter | solution.py:258
Sparse Core Ops, SparseCore 0:
  11.1 121.8 reduce-scatter.2
  136.9 216.8 all-gather.6
  355.7 228.9 all-gather.10
  587.0 227.7 all-gather.8
  885.7 259.7 reduce-scatter.4

commit v2 on v1

--- a/solution.py
+++ b/solution.py
@@ -1,3 +1,5 @@
+import functools
+
 import jax
 import jax.numpy as jnp
 from jax import lax
@@ -8,6 +10,7 @@
 DECAY = 0.99
 SHRINKAGE = 0.1
 EPSILON = 1e-06
+DEPTHS = (4, 5, 6, 7, 8)
 VMEM = 56 * 1024 * 1024
 
 
@@ -24,16 +27,20 @@
     return (slot_rank, filled, block_ids)
 
 
-def pick_body(row, col, live, all_ref, out_ref, sq_ref):
+def pick_body(row, rank, live, got_ref, out_ref, sq_ref):
     s = pl.program_id(0)
-    per_row, _, rows, quarter = all_ref.shape
+    cores, chips, _, rows, quarter = got_ref.shape
 
     @pl.when(live[s] > 0)
     def _():
-        block = all_ref[...].reshape(per_row * rows, quarter)
-        out_ref[0] = block
-        wide = block.astype(jnp.float32)
-        sq_ref[0] = jnp.sum(wide * wide, axis=0, keepdims=True)
+        total = jnp.zeros((1, quarter), jnp.float32)
+        for t in range(chips):
+            for c in range(cores):
+                part = got_ref[c, t, 0]
+                out_ref[0, pl.ds((t * cores + c) * rows, rows), :] = part
+                wide = part.astype(jnp.float32)
+                total = total + jnp.sum(wide * wide, axis=0, keepdims=True)
+        sq_ref[0] = total
 
     @pl.when(live[s] == 0)
     def _():
@@ -41,9 +48,10 @@
         sq_ref[...] = jnp.zeros_like(sq_ref)
 
 
-def pick_blocks(shards, row, col, live, per_row):
-    workers, ncols, rows, quarter = shards.shape
+def pick_blocks(got, row, rank, live, size):
+    cores, _, _, rows, quarter = got.shape
     slots = row.shape[0]
+    chips = size // (rows * cores)
     return pl.pallas_call(
         pick_body,
         grid_spec=pltpu.PrefetchScalarGridSpec(
@@ -51,21 +59,144 @@
             grid=(slots,),
             in_specs=[
                 pl.BlockSpec(
-                    (per_row, 1, rows, quarter), lambda s, row, col, live: (row[s], col[s], 0, 0)
+                    (cores, chips, 1, rows, quarter),
+                    lambda s, row, rank, live: (0, row[s], rank[s], 0, 0),
                 )
             ],
             out_specs=[
-                pl.BlockSpec((1, per_row * rows, quarter), lambda s, *_: (s, 0, 0)),
+                pl.BlockSpec((1, size, quarter), lambda s, *_: (s, 0, 0)),
                 pl.BlockSpec((1, 1, quarter), lambda s, *_: (s, 0, 0)),
             ],
         ),
         out_shape=[
-            jax.ShapeDtypeStruct((slots, per_row * rows, quarter), jnp.bfloat16),
+            jax.ShapeDtypeStruct((slots, size, quarter), jnp.bfloat16),
             jax.ShapeDtypeStruct((slots, 1, quarter), jnp.float32),
         ],
         compiler_params=pltpu.CompilerParams(vmem_limit_bytes=VMEM),
         name="pick_blocks",
-    )(row, col, live, shards)
+    )(row, rank, live, got)
+
+
+def fill_body(col, in_ref, out_ref):
+    out_ref[0] = in_ref[...]
+
+
+def fill_outgoing(by_block, col, chips, depth):
+    ncols, rows, quarter = by_block.shape
+    return pl.pallas_call(
+        fill_body,
+        grid_spec=pltpu.PrefetchScalarGridSpec(
+            num_scalar_prefetch=1,
+            grid=(chips, depth),
+            in_specs=[pl.BlockSpec((1, rows, quarter), lambda p, k, col: (col[p, k], 0, 0))],
+            out_specs=pl.BlockSpec((1, 1, rows, quarter), lambda p, k, *_: (p, k, 0, 0)),
+        ),
+        out_shape=jax.ShapeDtypeStruct((chips, depth, rows, quarter), jnp.bfloat16),
+        compiler_params=pltpu.CompilerParams(vmem_limit_bytes=VMEM),
+        name="fill_outgoing",
+    )(col, by_block)
+
+
+def exchange_body(
+    chips, depth, share, src, dst, own_sem, send_sem, recv_sem, pass_send, pass_recv
+):
+    rep = lax.axis_index("replica")
+    work = lax.axis_index("fsdp")
+    chip = work // 2
+    core = work % 2
+    sibling = (rep, chip * 2 + 1 - core)
+    part = pl.ds(0, depth)
+
+    def landing(p):
+        return dst.at[core, p, part] if share else dst.at[p, part]
+
+    def peer(d):
+        return lax.rem(chip + d, chips)
+
+    barrier = pltpu.get_barrier_semaphore()
+    for d in range(1, chips):
+        pl.semaphore_signal(
+            barrier, inc=1, device_id=(rep, peer(d) * 2 + core),
+            device_id_type=pl.DeviceIdType.MESH,
+        )
+    if share:
+        pl.semaphore_signal(
+            barrier, inc=1, device_id=sibling, device_id_type=pl.DeviceIdType.MESH
+        )
+    pl.semaphore_wait(barrier, chips if share else chips - 1)
+
+    sends = []
+    for d in range(1, chips):
+        copy = pltpu.make_async_remote_copy(
+            src_ref=src.at[peer(d), part],
+            dst_ref=landing(chip),
+            send_sem=send_sem.at[d],
+            recv_sem=recv_sem.at[d],
+            device_id=(rep, peer(d) * 2 + core),
+            device_id_type=pl.DeviceIdType.MESH,
+        )
+        copy.start()
+        sends.append(copy)
+    keep = pltpu.make_async_copy(src.at[chip, part], landing(chip), own_sem)
+    keep.start()
+    passes = []
+    if share:
+        copy = pltpu.make_async_remote_copy(
+            src_ref=src.at[chip, part],
+            dst_ref=landing(chip),
+            send_sem=pass_send.at[0],
+            recv_sem=pass_recv.at[0],
+            device_id=sibling,
+            device_id_type=pl.DeviceIdType.MESH,
+        )
+        copy.start()
+        passes.append(copy)
+    for d in range(1, chips):
+        sends[d - 1].wait_recv()
+        if share:
+            origin = lax.rem(chip + chips - d, chips)
+            copy = pltpu.make_async_remote_copy(
+                src_ref=landing(origin),
+                dst_ref=landing(origin),
+                send_sem=pass_send.at[d],
+                recv_sem=pass_recv.at[d],
+                device_id=sibling,
+                device_id_type=pl.DeviceIdType.MESH,
+            )
+            copy.start()
+            passes.append(copy)
+    keep.wait()
+    for copy in sends:
+        copy.wait_send()
+    for copy in passes:
+        copy.wait()
+
+
+def exchange(outgoing, most, share, name_id):
+    chips, depth, rows, quarter = outgoing.shape
+    shape = (chips, most, rows, quarter)
+    if share:
+        shape = (2,) + shape
+    return pl.pallas_call(
+        functools.partial(exchange_body, chips, depth, share),
+        out_shape=jax.ShapeDtypeStruct(shape, jnp.bfloat16),
+        in_specs=[pl.BlockSpec(memory_space=pl.ANY)],
+        out_specs=pl.BlockSpec(memory_space=pl.ANY),
+        scratch_shapes=[
+            pltpu.SemaphoreType.DMA,
+            pltpu.SemaphoreType.DMA((chips,)),
+            pltpu.SemaphoreType.DMA((chips,)),
+            pltpu.SemaphoreType.DMA((chips,)),
+            pltpu.SemaphoreType.DMA((chips,)),
+        ],
+        compiler_params=pltpu.CompilerParams(
+            collective_id=name_id, has_side_effects=True, vmem_limit_bytes=VMEM
+        ),
+        cost_estimate=pl.CostEstimate(
+            flops=0, bytes_accessed=64 * outgoing.size, transcendentals=0
+        ),
+        name="exchange_in" if share else "exchange_back",
+    )(outgoing)
 
 
 def step_body(
@@ -163,37 +294,66 @@
     )(ints, lscale, rscale, width, g_all, l_all, right_root, left_stat, right_stat)
 
 
-def spread_body(slot, mine, scale, pre_ref, out_ref):
-    b = pl.program_id(0)
-    per_row, _, rows, quarter = out_ref.shape
-
-    @pl.when(mine[b] > 0)
-    def _():
-        block = pre_ref[0].astype(jnp.float32) * scale[slot[b]]
-        out_ref[...] = block.astype(jnp.bfloat16).reshape(out_ref.shape)
-
-    @pl.when(mine[b] == 0)
-    def _():
-        out_ref[...] = jnp.zeros_like(out_ref)
-
-
-def spread_blocks(precond, slot, mine, scale, workers, ncols, rows):
-    slots, size, quarter = precond.shape
-    per_row = size // rows
-    return pl.pallas_call(
-        spread_body,
+def load_body(slot, own, core, own_ref, sib_ref, out_ref):
+    p, k = pl.program_id(0), pl.program_id(1)
+
+    @pl.when(own[p, k] > 0)
+    def _():
+        out_ref[0, 0] = own_ref[0, 0, 0]
+
+    @pl.when(own[p, k] == 0)
+    def _():
+        out_ref[0, 0] = sib_ref[0, 0]
+
+
+def load_outgoing(mine, sibling, slot, own, core, chips, depth):
+    _, hosts, _, rows, quarter = mine.shape
+    return pl.pallas_call(
+        load_body,
         grid_spec=pltpu.PrefetchScalarGridSpec(
             num_scalar_prefetch=3,
-            grid=(slot.shape[0],),
-            in_specs=[pl.BlockSpec((1, size, quarter), lambda b, slot, *_: (slot[b], 0, 0))],
-            out_specs=pl.BlockSpec(
-                (per_row, 1, rows, quarter), lambda b, *_: (b // ncols, b % ncols, 0, 0)
-            ),
-        ),
-        out_shape=jax.ShapeDtypeStruct((workers, ncols, rows, quarter), jnp.bfloat16),
+            grid=(chips, depth),
+            in_specs=[
+                pl.BlockSpec(
+                    (1, 1, 1, rows, quarter),
+                    lambda p, k, slot, own, core: (slot[p, k], p % hosts, core[0], 0, 0),
+                ),
+                pl.BlockSpec(
+                    (1, 1, rows, quarter),
+                    lambda p, k, slot, own, core: (slot[p, k], p % hosts, 0, 0),
+                ),
+            ],
+            out_specs=pl.BlockSpec((1, 1, rows, quarter), lambda p, k, *_: (p, k, 0, 0)),
+        ),
+        out_shape=jax.ShapeDtypeStruct((chips, depth, rows, quarter), jnp.bfloat16),
         compiler_params=pltpu.CompilerParams(vmem_limit_bytes=VMEM),
-        name="spread_blocks",
-    )(slot, mine, scale, precond)
+        name="load_outgoing",
+    )(slot, own, core, mine, sibling)
+
+
+def assemble_body(chip, rank, scale, in_ref, out_ref):
+    j = pl.program_id(0)
+    out_ref[0] = (in_ref[0, 0].astype(jnp.float32) * scale[j]).astype(jnp.bfloat16)
+
+
+def assemble(got, chip, rank, scale):
+    _, _, rows, quarter = got.shape
+    return pl.pallas_call(
+        assemble_body,
+        grid_spec=pltpu.PrefetchScalarGridSpec(
+            num_scalar_prefetch=3,
+            grid=(chip.shape[0],),
+            in_specs=[
+                pl.BlockSpec(
+                    (1, 1, rows, quarter), lambda j, chip, rank, scale: (chip[j], rank[j], 0, 0)
+                )
+            ],
+            out_specs=pl.BlockSpec((1, rows, quarter), lambda j, *_: (j, 0, 0)),
+        ),
+        out_shape=jax.ShapeDtypeStruct((chip.shape[0], rows, quarter), jnp.bfloat16),
+        compiler_params=pltpu.CompilerParams(vmem_limit_bytes=VMEM),
+        name="assemble",
+    )(chip, rank, scale, got)
 
 
 def on_device(grad_parts, col_widths, assignment, left_stat, right_stat, left_root, right_root):
@@ -203,7 +363,41 @@
     slots, quarter, block_size = left_stat.shape
     rows_dev, ncols = grad_parts.shape[1:3]
     per_row = block_size // rows_dev
+    chips = workers // 2
+    hosts = per_row // 2
+    chip, core = me_work // 2, me_work % 2
+    most = min(ncols, 2 * slots)
+    cases = [k for k in DEPTHS if k < most] + [most]
     slot_rank, filled, block_ids = slot_tables(assignment, workers, slots)
+    blocks = jnp.arange(assignment.shape[0], dtype=jnp.int32)
+    of_row = blocks // ncols
+    of_chip = assignment // 2
+    pair = of_row * chips + of_chip
+    pair_rank = jnp.sum(
+        ((pair[:, None] == pair[None, :]) & (blocks[None, :] < blocks[:, None])).astype(jnp.int32),
+        axis=1,
+    )
+    depth = jnp.max(pair_rank) + 1
+    case = sum((depth > k).astype(jnp.int32) for k in cases[:-1]) if len(cases) > 1 else None
+    owner_first = me_work // per_row * ncols
+    row_chip = lax.dynamic_slice_in_dim(of_chip, owner_first, ncols)
+    row_rank = lax.dynamic_slice_in_dim(pair_rank, owner_first, ncols)
+    all_chips = jnp.arange(chips, dtype=jnp.int32)
+    ranks = jnp.arange(most, dtype=jnp.int32)
+    leaves = (row_chip == all_chips[:, None, None]) & (row_rank == ranks[None, :, None])
+    send_col = jnp.sum(jnp.where(leaves, jnp.arange(ncols, dtype=jnp.int32), 0), axis=2)
+    returns = (
+        (of_chip == chip)
+        & (of_row == (all_chips // hosts)[:, None, None])
+        & (pair_rank == ranks[None, :, None])
+    )
+    back_slot = jnp.sum(jnp.where(returns, slot_rank, 0), axis=2)
+    back_own = jnp.sum((returns & (assignment == me_work)).astype(jnp.int32), axis=2)
+
+    def by_depth(make, *args):
+        if len(cases) == 1:
+            return make(0, *args)
+        return lax.switch(case, [functools.partial(make, n) for n in range(len(cases))], *args)
 
     summed = lax.psum_scatter(grad_parts[0], "replica", scatter_dimension=2, tiled=True)
     left_wide = lax.all_gather(left_root, "replica", axis=0)
@@ -232,8 +426,14 @@
 
     col_mask = global_rows[None, :] < col_widths[:, None]
     masked = jnp.where(col_mask[None], summed, jnp.zeros((), jnp.bfloat16))
-    shards = lax.all_gather(jnp.transpose(masked, (1, 0, 2)), "fsdp", axis=0)
-    g_cols, g_sq = pick_blocks(shards, my_row, my_col, my_filled.astype(jnp.int32), per_row)
+
+    def send_in(n, by_block, col):
+        outgoing = fill_outgoing(by_block, col, chips, cases[n])
+        return exchange(outgoing, most, True, 2 * n)
+
+    got = by_depth(send_in, jnp.transpose(masked, (1, 0, 2)), send_col)
+    my_rank = jnp.take(pair_rank, my_blocks)
+    g_cols, g_sq = pick_blocks(got, my_row, my_rank, my_filled.astype(jnp.int32), block_size)
     g_all = lax.all_gather(g_cols, "replica", axis=0)
     left_trace, right_trace, grad_square = lax.psum(
         (left_part, right_part, jnp.sum(g_sq, axis=(1, 2))), "replica"
@@ -248,14 +448,23 @@
     left_new, right_new, precond, p_sq = step_slots(
         ints, left_scale, right_scale, my_width, g_all, left_wide, right_root, left_stat, right_stat
     )
+    split = precond.reshape(slots, hosts, 2, rows_dev, quarter)
+    swap = [(w, w + 1 - 2 * (w % 2)) for w in range(workers)]
+    crossing = lax.dynamic_index_in_dim(split, 1 - core, 2, keepdims=False)
+    sibling = lax.ppermute(crossing, "fsdp", swap)
+
+    def send_back(n, mine, other, slot, own, core):
+        outgoing = load_outgoing(mine, other, slot, own, core, chips, cases[n])
+        return exchange(outgoing, most, False, 2 * n + 1)
+
+    back = by_depth(send_back, split, sibling, back_slot, back_own, core[None])
     precond_square = lax.psum(jnp.sum(p_sq, axis=(1, 2)), "replica")
     graft_scale = jnp.sqrt(grad_square / (precond_square + EPSILON))
-
-    mine = (assignment == me_work).astype(jnp.int32)
-    outgoing = spread_blocks(
-        precond, jnp.where(mine > 0, slot_rank, 0), mine, graft_scale, workers, ncols, rows_dev
-    )
-    arrived = lax.psum_scatter(outgoing, "fsdp", scatter_dimension=0, tiled=False)
+    every_scale = lax.all_gather(graft_scale, "fsdp", axis=0, tiled=True)
+    owner_worker = lax.dynamic_slice_in_dim(assignment, owner_first, ncols)
+    owner_slot = lax.dynamic_slice_in_dim(slot_rank, owner_first, ncols)
+    my_scale = jnp.take(every_scale, owner_worker * slots + owner_slot)
+    arrived = assemble(back, row_chip, row_rank, my_scale)
     update = jnp.transpose(arrived, (1, 0, 2))
     return (update, left_new, right_new)
 

time: 1160 us -> 854 us (0.74); the launches traced: 1150 us -> 863 us
  waiting for transfers between devices: 1030 us -> 376 us
  Pallas kernels: 69 us -> 421 us
    pallas_call x1 -> x5, Pallas kernels: 25.6 us -> 362 us  [the longest x2 325 us: exchange(): pl.pallas_call(functools.partial(exchange_body, chips, depth, share), out...]
    reduce_scatter x1 -> x0, waiting for transfers between devices: 260 us -> none  [on_device(): lax.psum_scatter(outgoing, 'fsdp', scatter_dimension=0, tiled=False)]
    all_gather x1 -> x0, waiting for transfers between devices: 213 us -> none  [on_device(): shards = lax.all_gather(jnp.transpose(masked, (1, 0, 2)), 'fsdp', axis=0)]
    all_gather x1, waiting for transfers between devices: 204 us -> 26.2 us  [on_device(): left_wide = lax.all_gather(left_root, 'replica', axis=0)]
    pallas_call x1, Pallas kernels: 34.9 us -> 49.5 us  [step_slots(): pl.pallas_call(step_body, grid_spec=pltpu.PrefetchScalarGridSpec(num_scal...]
  transfers between devices with their start and end apart: 5 -> 4, of which waited for: 5 -> 3; matrix products, arithmetic and copies ran while one was open for 1% -> 2% of each run, Pallas kernels for 1% -> 22%
where the time goes in v2:
time: 854 us; the launch traced here: 863 us
  Pallas kernels  421 us (49%)
  waiting for transfers between devices  376 us (44%)
  blocking collectives  28.1 us (3%)
  between operations  15.3 us (2%)
  other arithmetic  14.1 us (2%)
    pallas_call x2, Pallas kernels, exchange(): pl.pallas_call(functools.partial(exchange_body, chips, depth, share), out...  325 us
    all_gather x1, waiting for transfers between devices, on_device(): g_all = lax.all_gather(g_cols, 'replica', axis=0)  230 us
    reduce_scatter x1, waiting for transfers between devices, on_device(): lax.psum_scatter(grad_parts[0], 'replica', scatter_dimension=2, tiled=True)  119 us
    pallas_call x1, Pallas kernels, step_slots(): pl.pallas_call(step_body, grid_spec=pltpu.PrefetchScalarGridSpec(num_scal...  49.5 us
    all_gather x1, waiting for transfers between devices, on_device(): left_wide = lax.all_gather(left_root, 'replica', axis=0)  26.2 us
    pallas_call x1, Pallas kernels, load_outgoing(): pl.pallas_call(load_body, grid_spec=pltpu.PrefetchScalarGridSpec(num_scal...  17.2 us
  transfers between devices with their start and end apart: 4, of which 3 were waited for; matrix products, arithmetic and copies ran while one was open for 2% of the time, Pallas kernels for 22%

profile of v2, /device:TPU:8, one launch (start us, length us, event | category | flops | bytes accessed | tf_op | source)
XLA Modules:
  0.0 863.5 jit_solution(1671634332242775874)
XLA Ops:
  7.2 0.0 reduce-scatter.2.cloned.1.call-start
  7.2 0.0 copy-start.3
  7.2 0.0 copy-start.5
  7.2 0.7 reduce-scatter.2.cloned.1.call-update
  7.9 0.0 all-gather.7.cloned.1.call-start
  7.9 0.7 all-gather.7.cloned.1.call-update
  8.6 0.0 all-gather.5.cloned.1.call-start
  8.7 0.0 copy-done.3
  8.7 0.1 dynamic_slice.28.chip
  8.8 0.0 copy-start.4
  8.8 0.2 convert_reduce_fusion.3
  9.0 0.1 dynamic_slice.29.rank
  9.1 0.0 copy-start.2
  9.1 0.6 reduce_max.9
  10.4 0.2 convert_reduce_fusion.2
  10.6 0.1 convert_reduce_fusion.1
  10.7 0.6 and_select_fusion.1
  11.3 0.7 gather_fusion
  12.0 0.3 select_reduce_fusion
  12.3 0.0 copy-done.5
  12.3 0.2 select_reduce_fusion.3
  12.5 0.0 copy-done.4
  12.5 0.5 and_select_fusion.2.rank
  13.0 1.3 fusion.5
  14.4 0.1 broadcast_compare_fusion
  14.4 0.0 copy-done.2
  14.4 118.6 %reduce-scatter.2.cloned.1.call-done = bf16[512,12,256]{2,0,1:T(8,128)(2,1)} async-done(((bf16[512,12,1024]{2,0,1:T(8,128)(2,1)}), bf16[512,12,256]{2,0,1:T(8,128)(2,1)}) %reduce-scatter.2.cloned.1.call-update) | async-done | bytes 3145744 | tf_op jit(solution)/shard_map/reduce_scatter | solution.py:402
  133.1 2.1 select_bitcast_fusion
  135.2 176.5 %conditional.2 = (bf16[2,4,12,512,256]{4,3,2,1,0:T(8,128)(2,1)}) conditional(s32[]{:T(128)} %clamp.4, (s32[4,12]{0,1:T(8,128)S(1)}, bf16[12,512,256]{2,1,0:T(8,128)(2,1)S(1)}) %tuple.44, (s32[4,12]{0,1:T(8,128)S(1)}, bf16[12,512,256]{2,1,0:T(8,128)(2,1)S(1)}) %tuple.44, (s32[4,12]{0,1:T(8,128)S(1)}, ...), branch_computations={%region_7.8_spmd, %region_8.9_spmd, %region_9.10_spmd, %region_10.... | conditional | bytes 402653568 | solution.py:400
  135.2 0.7 copy.31.col
  135.9 10.9 %fill_outgoing.9.src = bf16[4,7,512,256]{3,2,1,0:T(8,128)(2,1)} custom-call(s32[4,12]{1,0:T(4,128)} %copy.31.col, bf16[12,512,256]{2,1,0:T(8,128)(2,1)S(1)} %get-tuple-element.99.in_ref), custom_call_target="tpu_custom_call" | custom-call | tf_op jit(solution)/shard_map/cond/branch_3_fun/fill_outgoing/pallas_call | solution.py:86
  146.7 164.9 %exchange_in.9 = bf16[2,4,12,512,256]{4,3,2,1,0:T(8,128)(2,1)} custom-call(bf16[4,7,512,256]{3,2,1,0:T(8,128)(2,1)} %fill_outgoing.9.src), custom_call_target="tpu_custom_call" | custom-call | bytes 234881024 | tf_op jit(solution)/shard_map/cond/branch_3_fun/exchange_in/pallas_call | solution.py:180
  311.7 10.1 %pick_blocks.1 = (bf16[12,1024,256]{2,1,0:T(8,128)(2,1)}, f32[12,1,256]{2,1,0:T(1,128)}) custom-call(s32[12]{0:T(128)} %get-tuple-element.305.row, s32[12]{0:T(128)} %and_select_fusion.2.rank, s32[12]{0:T(128)} %get-tuple-element.299.live, bf16[2,4,12,512,256]{4,3,2,1,0:T(8,128)(2,1)} %get-tuple-element.309.got_ref), custom_call_target="tpu_custom_call" | custom-call | tf_op jit(solution)/shard_map/pick_blocks/pallas_call | solution.py:55
  321.7 0.0 all-gather.5.cloned.1.call-update
  321.8 1.3 pad_add_fusion.ints
  323.0 3.6 multiply_reduce_fusion
  326.7 0.2 select_reduce_fusion.2
  326.9 0.0 copy-done
  326.9 0.2 reduce_sum.135
  327.0 9.2 %all-reduce.1 = (f32[12]{0:T(128)S(1)}, f32[12]{0:T(128)S(1)}, f32[12]{0:T(128)S(1)}) all-reduce(f32[12]{0:T(128)S(1)} %reduce_sum.135, f32[12]{0:T(128)S(1)} %get-tuple-element.288, f32[12]{0:T(128)S(1)} %select_reduce_fusion.2), channel_id=1, replica_groups=mesh['replica'=4,'fsdp'=8] {'replica'}, use_global_device_ids=true, to_apply=%region_14.15 | all-reduce | flops 36 | bytes 288 | tf_op jit(solution)/shard_map/psum | solution.py:438
  336.2 0.0 copy-done.1
  336.2 0.5 convert_divide_fusion
  336.7 26.2 %all-gather.7.cloned.1.call-done = bf16[48,1024,256]{2,1,0:T(8,128)(2,1)} async-done(((bf16[12,1024,256]{2,1,0:T(8,128)(2,1)}), bf16[48,1024,256]{2,1,0:T(8,128)(2,1)}) %all-gather.7.cloned.1.call-update) | async-done | bytes 25165840 | tf_op jit(solution)/shard_map/all_gather | solution.py:403
  362.9 230.2 %all-gather.5.cloned.1.call-done = bf16[48,1024,256]{2,1,0:T(8,128)(2,1)} async-done(((bf16[12,1024,256]{2,1,0:T(8,128)(2,1)}), bf16[48,1024,256]{2,1,0:T(8,128)(2,1)}) %all-gather.5.cloned.1.call-update) | async-done | bytes 25165840 | tf_op jit(solution)/shard_map/all_gather | solution.py:437
  593.1 49.5 %step_slots.1 = (f32[12,256,1024]{2,1,0:T(8,128)}, f32[12,256,1024]{2,1,0:T(8,128)}, bf16[12,1024,256]{2,1,0:T(8,128)(2,1)}, f32[12,1,256]{2,1,0:T(1,128)}) custom-call(s32[2]{0:T(128)} %pad_add_fusion.ints, f32[12]{0:T(128)} %get-tuple-element.302.lscale, f32[12]{0:T(128)} %get-tuple-element.301.rscale, s32[12]{0:T(128)} %copy-done.1, ...), custom_call_target="tpu_custom_call" | custom-call | tf_op jit(solution)/shard_map/step_slots/pallas_call | solution.py:273
  642.6 3.8 dynamic-slice_bitcast_fusion
  646.4 0.0 collective-permute-start
  646.4 0.0 copy-done.6
  646.4 0.7 dynamic-slice
  647.0 0.1 compare_select_fusion.1
  647.1 0.5 convert_reduce_fusion
  647.6 0.9 reduce_sum.141
  649.2 9.0 %psum.31 = f32[12]{0:T(128)S(1)} all-reduce(f32[12]{0:T(128)S(1)} %reduce_sum.141), channel_id=1, replica_groups=mesh['replica'=4,'fsdp'=8] {'replica'}, use_global_device_ids=true, to_apply=%region_23.24 | all-reduce | flops 12 | bytes 96 | tf_op jit(solution)/shard_map/psum | solution.py:461
  658.2 0.1 sqrt_dynamic-update-slice_fusion
  658.3 10.0 %all-reduce = f32[96]{0:T(128)S(1)} all-reduce(f32[96]{0:T(128)S(1)} %sqrt_dynamic-update-slice_fusion), channel_id=1, replica_groups=mesh['replica'=4,'fsdp'=8] {'fsdp'}, use_global_device_ids=true, to_apply=%add | all-reduce | flops 96 | bytes 768
  668.3 0.7 gather_fusion.1
  668.9 0.5 and_select_fusion.4.scale
  669.4 0.0 collective-permute-done
  669.4 178.8 %conditional.3 = (bf16[4,12,512,256]{3,2,1,0:T(8,128)(2,1)}) conditional(s32[]{:T(128)} %clamp.4, (s32[4,12]{0,1:T(8,128)S(1)}, s32[4,12]{0,1:T(8,128)S(1)}, s32[1]{0:T(128)}, bf16[12,1,2,512,256]{4,3,2,0,1:T(8,128)(2,1)}, bf16[12,1,512,256]{3,2,1,0:T(8,128)(2,1)S(1)}) %tuple.106, (s32[4,12]{0,1:T(8,128)S(1)}, ...), branch_computations={%region_26.27_spmd, %region_27.28_spmd, %region_28.29_spmd, %regio... | conditional | bytes 402653952 | solution.py:400
  669.4 0.7 copy.43.slot
  670.1 0.7 copy.44.own
  670.7 17.2 %load_outgoing.9.src = bf16[4,7,512,256]{3,2,1,0:T(8,128)(2,1)} custom-call(s32[4,12]{1,0:T(4,128)} %copy.43.slot, s32[4,12]{1,0:T(4,128)} %copy.44.own, s32[1]{0:T(128)} %get-tuple-element.127.core, bf16[12,1,2,512,256]{4,3,2,1,0:T(8,128)(2,1)} %bitcast.29, bf16[12,1,512,256]{3,2,1,0:T(8,128)(2,1)S(1)} %get-tuple-element.129.sib_ref), custom_call_target="tpu_custom_call" | custom-call | tf_op jit(solution)/shard_map/cond/branch_3_fun/load_outgoing/pallas_call | solution.py:311
  687.9 160.3 %exchange_back.9 = bf16[4,12,512,256]{3,2,1,0:T(8,128)(2,1)} custom-call(bf16[4,7,512,256]{3,2,1,0:T(8,128)(2,1)} %load_outgoing.9.src), custom_call_target="tpu_custom_call" | custom-call | bytes 234881024 | tf_op jit(solution)/shard_map/cond/branch_3_fun/exchange_back/pallas_call | solution.py:180
  848.2 8.7 %assemble.1 = bf16[12,512,256]{2,1,0:T(8,128)(2,1)} custom-call(s32[12]{0:T(128)} %copy-done.4, s32[12]{0:T(128)} %copy-done.2, f32[12]{0:T(128)} %and_select_fusion.4.scale, bf16[4,12,512,256]{3,2,1,0:T(8,128)(2,1)} %get-tuple-element.310.in_ref), custom_call_target="tpu_custom_call" | custom-call | tf_op jit(solution)/shard_map/assemble/pallas_call | solution.py:341
  (16 shorter events, 0.1 us)
Async XLA Ops:
  7.2 125.9 %reduce-scatter.2.cloned.1.call-start = ((), (), s32[]{:S(2)}) async-start(), calls=%async_computation.1 | async-start | bytes 15728640 | tf_op jit(solution)/shard_map/reduce_scatter | solution.py:402
  7.2 1.5 copy-start.3
  7.2 5.1 copy-start.5
  7.9 355.0 %all-gather.7.cloned.1.call-start = ((), (), s32[]{:S(2)}) async-start(), calls=%async_computation.3 | async-start | bytes 31457280 | tf_op jit(solution)/shard_map/all_gather | solution.py:403
  8.6 584.5 %all-gather.5.cloned.1.call-start = ((), (), s32[]{:S(2)}) async-start(), calls=%async_computation.2 | async-start | bytes 31457280 | tf_op jit(solution)/shard_map/all_gather | solution.py:437
  8.8 3.7 copy-start.4
  9.1 5.3 copy-start.2
  14.4 321.8 %copy-start.1 = (s32[12]{0:T(128)}, s32[12]{0:T(128)S(1)}, u32[]{:S(2)}) copy-start(s32[12]{0:T(128)S(1)} %get-tuple-element.303.width) | copy-start | bytes 148
  321.7 5.1 copy-start
  593.1 53.3 %copy-start.6 = (u32[32]{0:T(128)S(1)}, u32[32]{0:T(128)}, u32[]{:S(2)}) copy-start(u32[32]{0:T(128)} %constant.157) | copy-start | bytes 388
  646.4 23.1 %collective-permute-start = (bf16[12,1,512,256]{3,2,1,0:T(8,128)(2,1)}, bf16[12,1,512,256]{3,2,1,0:T(8,128)(2,1)S(1)}, u32[]{:S(2)}, u32[]{:S(2)}) collective-permute-start(bf16[12,1,512,256]{3,2,1,0:T(8,128)(2,1)} %dynamic-slice_bitcast_fusion), channel_id=1, source_target_pairs={{0,1},{1,0},{2,3},{3,2},{4,5},{5,4},{6,7},{7,6},{8,9},{9,8},{10,11... | collective-permute-start | bytes 9437192 | tf_op jit(solution)/shard_map/ppermute | solution.py:454
Sparse Core Ops, SparseCore 0:
  11.1 121.9 reduce-scatter.1
  134.9 227.9 all-gather.6
  365.4 227.7 all-gather.4

commit v3 on v2

--- a/solution.py
+++ b/solution.py
@@ -10,7 +10,9 @@
 DECAY = 0.99
 SHRINKAGE = 0.1
 EPSILON = 1e-06
-DEPTHS = (4, 5, 6, 7, 8)
+DEPTHS = (4, 5, 6, 8)
+WIDTHS = (8, 9, 10)
+REPLICAS = 4
 VMEM = 56 * 1024 * 1024
 
 
@@ -27,41 +29,49 @@
     return (slot_rank, filled, block_ids)
 
 
-def pick_body(row, rank, live, got_ref, out_ref, sq_ref):
+def pick_body(row, rank, live, own_row, own_rank, own_live, got_ref, own_ref, out_ref, sq_ref):
     s = pl.program_id(0)
     cores, chips, _, rows, quarter = got_ref.shape
 
     @pl.when(live[s] > 0)
+    def _():
+        for t in range(chips):
+            for c in range(cores):
+                out_ref[0, pl.ds((t * cores + c) * rows, rows), :] = got_ref[c, t, 0]
+
+    @pl.when(live[s] == 0)
+    def _():
+        out_ref[...] = jnp.zeros_like(out_ref)
+
+    @pl.when(own_live[s] > 0)
     def _():
         total = jnp.zeros((1, quarter), jnp.float32)
         for t in range(chips):
             for c in range(cores):
-                part = got_ref[c, t, 0]
-                out_ref[0, pl.ds((t * cores + c) * rows, rows), :] = part
-                wide = part.astype(jnp.float32)
+                wide = own_ref[c, t, 0].astype(jnp.float32)
                 total = total + jnp.sum(wide * wide, axis=0, keepdims=True)
         sq_ref[0] = total
 
-    @pl.when(live[s] == 0)
-    def _():
-        out_ref[...] = jnp.zeros_like(out_ref)
+    @pl.when(own_live[s] == 0)
+    def _():
         sq_ref[...] = jnp.zeros_like(sq_ref)
 
 
-def pick_blocks(got, row, rank, live, size):
+def pick_blocks(got, wire, own, size):
     cores, _, _, rows, quarter = got.shape
-    slots = row.shape[0]
+    slots = own[0].shape[0]
     chips = size // (rows * cores)
+    block = (cores, chips, 1, rows, quarter)
     return pl.pallas_call(
         pick_body,
         grid_spec=pltpu.PrefetchScalarGridSpec(
-            num_scalar_prefetch=3,
+            num_scalar_prefetch=6,
             grid=(slots,),
             in_specs=[
+                pl.BlockSpec(block, lambda s, row, rank, *_: (0, row[s], rank[s], 0, 0)),
                 pl.BlockSpec(
-                    (cores, chips, 1, rows, quarter),
-                    lambda s, row, rank, live: (0, row[s], rank[s], 0, 0),
-                )
+                    block, lambda s, a, b, c, row, rank, live: (0, row[s], rank[s], 0, 0)
+                ),
             ],
             out_specs=[
                 pl.BlockSpec((1, size, quarter), lambda s, *_: (s, 0, 0)),
@@ -74,7 +84,7 @@
         ],
         compiler_params=pltpu.CompilerParams(vmem_limit_bytes=VMEM),
         name="pick_blocks",
-    )(row, rank, live, got)
+    )(*wire, *own, got, got)
 
 
 def fill_body(col, in_ref, out_ref):
@@ -97,106 +107,261 @@
     )(col, by_block)
 
 
-def exchange_body(
-    chips, depth, share, src, dst, own_sem, send_sem, recv_sem, pass_send, pass_recv
-):
-    rep = lax.axis_index("replica")
-    work = lax.axis_index("fsdp")
-    chip = work // 2
-    core = work % 2
-    sibling = (rep, chip * 2 + 1 - core)
-    part = pl.ds(0, depth)
-
-    def landing(p):
-        return dst.at[core, p, part] if share else dst.at[p, part]
-
-    def peer(d):
-        return lax.rem(chip + d, chips)
-
+def remote(src, dst, sems, at, device):
+    return pltpu.make_async_remote_copy(
+        src_ref=src,
+        dst_ref=dst,
+        send_sem=sems[0].at[at],
+        recv_sem=sems[1].at[at],
+        device_id=device,
+        device_id_type=pl.DeviceIdType.MESH,
+    )
+
+
+def greet(devices):
     barrier = pltpu.get_barrier_semaphore()
-    for d in range(1, chips):
+    for device in devices:
         pl.semaphore_signal(
-            barrier, inc=1, device_id=(rep, peer(d) * 2 + core),
-            device_id_type=pl.DeviceIdType.MESH,
+            barrier, inc=1, device_id=device, device_id_type=pl.DeviceIdType.MESH
         )
-    if share:
-        pl.semaphore_signal(
-            barrier, inc=1, device_id=sibling, device_id_type=pl.DeviceIdType.MESH
-        )
-    pl.semaphore_wait(barrier, chips if share else chips - 1)
-
-    sends = []
-    for d in range(1, chips):
-        copy = pltpu.make_async_remote_copy(
-            src_ref=src.at[peer(d), part],
-            dst_ref=landing(chip),
-            send_sem=send_sem.at[d],
-            recv_sem=recv_sem.at[d],
-            device_id=(rep, peer(d) * 2 + core),
-            device_id_type=pl.DeviceIdType.MESH,
+    pl.semaphore_wait(barrier, len(devices))
+
+
+class Gather:
+    def __init__(self, wide, src, dst, own_sem, sems, tail_sems):
+        rep, work = lax.axis_index("replica"), lax.axis_index("fsdp")
+        self.wide, self.src, self.dst = wide, src, dst
+        self.own_sem, self.sems, self.tail_sems = own_sem, sems, tail_sems
+        self.rep = rep
+        across = rep // 2
+        along = rep % 2
+        self.x_rep = across * 2 + 1 - along
+        self.y_rep = (1 - across) * 2 + along
+        self.d_rep = (1 - across) * 2 + 1 - along
+        self.x = (self.x_rep, work)
+        self.y = (self.y_rep, work)
+        self.sibling = (rep, work // 2 * 2 + 1 - work % 2)
+        self.slots, self.size = src.shape[:2]
+
+    def devices(self):
+        return [self.x, self.y] + ([self.sibling] if self.wide < self.slots else [])
+
+    def half(self, ref, h):
+        mid = self.size // 2
+        return ref.at[pl.ds(0, self.wide), pl.ds(h * mid, mid)]
+
+    def start(self):
+        mine = self.dst.at[self.rep]
+        self.out = []
+        for at, (to, h) in enumerate([(self.x, 0), (self.y, 1), (self.x, 1), (self.y, 0)]):
+            copy = remote(self.half(self.src, h), self.half(mine, h), self.sems, at, to)
+            copy.start()
+            self.out.append(copy)
+        held = pl.ds(0, self.wide)
+        self.keep = pltpu.make_async_copy(self.src.at[held], mine.at[held], self.own_sem)
+        self.keep.start()
+        self.tails = []
+        self.tail(self.src, self.rep, 0)
+
+    def tail(self, shard, origin, at):
+        more = self.slots - self.wide
+        if more == 0:
+            return
+        copy = remote(
+            shard.at[pl.ds(self.wide - more, more)],
+            self.dst.at[origin, pl.ds(self.wide, more)],
+            self.tail_sems, at, self.sibling,
         )
         copy.start()
-        sends.append(copy)
-    keep = pltpu.make_async_copy(src.at[chip, part], landing(chip), own_sem)
-    keep.start()
-    passes = []
-    if share:
-        copy = pltpu.make_async_remote_copy(
-            src_ref=src.at[chip, part],
-            dst_ref=landing(chip),
-            send_sem=pass_send.at[0],
-            recv_sem=pass_recv.at[0],
-            device_id=sibling,
-            device_id_type=pl.DeviceIdType.MESH,
-        )
+        self.tails.append(copy)
+
+    def forward(self):
+        from_x, from_y = self.dst.at[self.x_rep], self.dst.at[self.y_rep]
+        self.out[0].wait_recv()
+        copy = remote(self.half(from_x, 0), self.half(from_x, 0), self.sems, 4, self.y)
         copy.start()
-        passes.append(copy)
-    for d in range(1, chips):
-        sends[d - 1].wait_recv()
-        if share:
-            origin = lax.rem(chip + chips - d, chips)
-            copy = pltpu.make_async_remote_copy(
-                src_ref=landing(origin),
-                dst_ref=landing(origin),
-                send_sem=pass_send.at[d],
-                recv_sem=pass_recv.at[d],
-                device_id=sibling,
-                device_id_type=pl.DeviceIdType.MESH,
-            )
+        self.out.append(copy)
+        self.out[1].wait_recv()
+        copy = remote(self.half(from_y, 1), self.half(from_y, 1), self.sems, 5, self.x)
+        copy.start()
+        self.out.append(copy)
+
+    def finish(self):
+        self.out[2].wait_recv()
+        self.tail(self.dst.at[self.x_rep], self.x_rep, 1)
+        self.out[3].wait_recv()
+        self.tail(self.dst.at[self.y_rep], self.y_rep, 2)
+        self.out[4].wait_recv()
+        self.out[5].wait_recv()
+        self.tail(self.dst.at[self.d_rep], self.d_rep, 3)
+        self.keep.wait()
+        for copy in self.out:
+            copy.wait_send()
+        for copy in self.tails:
+            copy.wait()
+
+
+class Exchange:
+    def __init__(self, chips, depth, share, src, dst, own_sem, sems, pass_sems):
+        rep, work = lax.axis_index("replica"), lax.axis_index("fsdp")
+        self.chips, self.depth, self.share = chips, depth, share
+        self.src, self.dst = src, dst
+        self.own_sem, self.sems, self.pass_sems = own_sem, sems, pass_sems
+        self.chip, self.core = work // 2, work % 2
+        self.rep = rep
+        self.sibling = (rep, self.chip * 2 + 1 - self.core)
+
+    def peer(self, d):
+        return lax.rem(self.chip + d, self.chips)
+
+    def device(self, d):
+        return (self.rep, self.peer(d) * 2 + self.core)
+
+    def devices(self):
+        peers = [self.device(d) for d in range(1, self.chips)]
+        return peers + ([self.sibling] if self.share else [])
+
+    def landing(self, p):
+        part = pl.ds(0, self.depth)
+        return self.dst.at[self.core, p, part] if self.share else self.dst.at[p, part]
+
+    def start(self):
+        here = self.landing(self.chip)
+        self.out = []
+        for d in range(1, self.chips):
+            copy = remote(self.src.at[self.peer(d)], here, self.sems, d, self.device(d))
             copy.start()
-            passes.append(copy)
-    keep.wait()
-    for copy in sends:
-        copy.wait_send()
-    for copy in passes:
-        copy.wait()
-
-
-def exchange(outgoing, most, share, name_id):
+            self.out.append(copy)
+        self.keep = pltpu.make_async_copy(self.src.at[self.chip], here, self.own_sem)
+        self.keep.start()
+        self.passes = []
+        if self.share:
+            copy = remote(self.src.at[self.chip], here, self.pass_sems, 0, self.sibling)
+            copy.start()
+            self.passes.append(copy)
+
+    def forward(self):
+        for d in range(1, self.chips):
+            self.out[d - 1].wait_recv()
+            if self.share:
+                came = self.landing(lax.rem(self.chip + self.chips - d, self.chips))
+                copy = remote(came, came, self.pass_sems, d, self.sibling)
+                copy.start()
+                self.passes.append(copy)
+
+    def finish(self):
+        self.keep.wait()
+        for copy in self.out:
+            copy.wait_send()
+        for copy in self.passes:
+            copy.wait()
+
+
+def pair_of(n):
+    return [pltpu.SemaphoreType.DMA((n,)), pltpu.SemaphoreType.DMA((n,))]
+
+
+def remote_call(body, shapes, scratch, collective_id, name, size):
+    anywhere = pl.BlockSpec(memory_space=pl.ANY)
+
+    def call(*args):
+        return pl.pallas_call(
+            body,
+            out_shape=[jax.ShapeDtypeStruct(shape, jnp.bfloat16) for shape in shapes],
+            in_specs=[anywhere] * len(args),
+            out_specs=[anywhere] * len(shapes),
+            scratch_shapes=scratch,
+            compiler_params=pltpu.CompilerParams(
+                collective_id=collective_id, has_side_effects=True, vmem_limit_bytes=VMEM
+            ),
+            cost_estimate=pl.CostEstimate(flops=0, bytes_accessed=size, transcendentals=0),
+            name=name,
+        )(*args)
+
+    return call
+
+
+def bring_in(outgoing, root, wide, most, collective_id):
     chips, depth, rows, quarter = outgoing.shape
-    shape = (chips, most, rows, quarter)
-    if share:
-        shape = (2,) + shape
+
+    def body(src, root_ref, dst, all_ref, own, ex_s, ex_r, pass_s, pass_r, ga_s, ga_r, ta_s, ta_r):
+        ex = Exchange(chips, depth, True, src, dst, own.at[0], (ex_s, ex_r), (pass_s, pass_r))
+        ga = Gather(wide, root_ref, all_ref, own.at[1], (ga_s, ga_r), (ta_s, ta_r))
+        others = ex.devices()
+        greet(others + ga.devices()[:2])
+        ex.start()
+        ga.start()
+        ga.forward()
+        ex.forward()
+        ga.finish()
+        ex.finish()
+
+    shapes = [(2, chips, most, rows, quarter), (REPLICAS,) + root.shape]
+    scratch = [pltpu.SemaphoreType.DMA((2,))]
+    scratch += pair_of(chips) + pair_of(chips) + pair_of(6) + pair_of(4)
+    size = 64 * outgoing.size
+    return remote_call(body, shapes, scratch, collective_id, "bring_in", size)(outgoing, root)
+
+
+def gather_slots(shard, wide, collective_id):
+    def body(src, dst, own, ga_s, ga_r, ta_s, ta_r):
+        ga = Gather(wide, src, dst, own, (ga_s, ga_r), (ta_s, ta_r))
+        greet(ga.devices())
+        ga.start()
+        ga.forward()
+        ga.finish()
+
+    scratch = [pltpu.SemaphoreType.DMA] + pair_of(6) + pair_of(4)
+    size = 16 * shard.size
+    shapes = [(REPLICAS,) + shard.shape]
+    return remote_call(body, shapes, scratch, collective_id, "gather_slots", size)(shard)[0]
+
+
+def send_home(outgoing, most, collective_id):
+    chips, depth, rows, quarter = outgoing.shape
+
+    def body(src, dst, own, ex_s, ex_r):
+        ex = Exchange(chips, depth, False, src, dst, own, (ex_s, ex_r), None)
+        greet(ex.devices())
+        ex.start()
+        ex.forward()
+        ex.finish()
+
+    scratch = [pltpu.SemaphoreType.DMA] + pair_of(chips)
+    size = 64 * outgoing.size
+    shapes = [(chips, most, rows, quarter)]
+    return remote_call(body, shapes, scratch, collective_id, "send_home", size)(outgoing)[0]
+
+
+def wire_body(own_at, sib_at, use_sib, own_ref, sib_ref, out_ref):
+    t = pl.program_id(0)
+
+    @pl.when(use_sib[t] > 0)
+    def _():
+        out_ref[...] = sib_ref[...]
+
+    @pl.when(use_sib[t] == 0)
+    def _():
+        out_ref[...] = own_ref[...]
+
+
+def wire_slots(own, sib, own_at, sib_at, use_sib):
+    block = (1,) + own.shape[1:]
     return pl.pallas_call(
-        functools.partial(exchange_body, chips, depth, share),
-        out_shape=jax.ShapeDtypeStruct(shape, jnp.bfloat16),
-        in_specs=[pl.BlockSpec(memory_space=pl.ANY)],
-        out_specs=pl.BlockSpec(memory_space=pl.ANY),
-        scratch_shapes=[
-            pltpu.SemaphoreType.DMA,
-            pltpu.SemaphoreType.DMA((chips,)),
-            pltpu.SemaphoreType.DMA((chips,)),
-            pltpu.SemaphoreType.DMA((chips,)),
-            pltpu.SemaphoreType.DMA((chips,)),
-        ],
-        compiler_params=pltpu.CompilerParams(
-            collective_id=name_id, has_side_effects=True, vmem_limit_bytes=VMEM
+        wire_body,
+        grid_spec=pltpu.PrefetchScalarGridSpec(
+            num_scalar_prefetch=3,
+            grid=(own.shape[0],),
+            in_specs=[
+                pl.BlockSpec(block, lambda t, own_at, sib_at, use_sib: (own_at[t], 0, 0)),
+                pl.BlockSpec(block, lambda t, own_at, sib_at, use_sib: (sib_at[t], 0, 0)),
+            ],
+            out_specs=pl.BlockSpec(block, lambda t, *_: (t, 0, 0)),
         ),
-        cost_estimate=pl.CostEstimate(
-            flops=0, bytes_accessed=64 * outgoing.size, transcendentals=0
-        ),
-        name="exchange_in" if share else "exchange_back",
-    )(outgoing)
+        out_shape=jax.ShapeDtypeStruct(own.shape, own.dtype),
+        compiler_params=pltpu.CompilerParams(vmem_limit_bytes=VMEM),
+        name="wire_slots",
+    )(own_at, sib_at, use_sib, own, sib)
 
 
 def step_body(
@@ -267,7 +432,11 @@
     def used(s, ints):
         return jnp.minimum(s, jnp.maximum(ints[1] - 1, 0))
 
-    gathered = pl.BlockSpec((n, 1, size, quarter), lambda s, ints, *_: (0, used(s, ints), 0, 0))
+    def held(s, ints):
+        at = used(s, ints)
+        return jnp.where(at < ints[2], at, at + slots - ints[1])
+
+    gathered = pl.BlockSpec((n, 1, size, quarter), lambda s, ints, *_: (0, held(s, ints), 0, 0))
     tall = pl.BlockSpec((1, size, quarter), lambda s, ints, *_: (used(s, ints), 0, 0))
     stat = pl.BlockSpec((1, quarter, size), lambda s, *_: (s, 0, 0))
     return pl.pallas_call(
@@ -368,6 +537,7 @@
     chip, core = me_work // 2, me_work % 2
     most = min(ncols, 2 * slots)
     cases = [k for k in DEPTHS if k < most] + [most]
+    widths = [k for k in WIDTHS if slots <= 2 * k and k < slots] + [slots]
     slot_rank, filled, block_ids = slot_tables(assignment, workers, slots)
     blocks = jnp.arange(assignment.shape[0], dtype=jnp.int32)
     of_row = blocks // ncols
@@ -378,7 +548,13 @@
         axis=1,
     )
     depth = jnp.max(pair_rank) + 1
-    case = sum((depth > k).astype(jnp.int32) for k in cases[:-1]) if len(cases) > 1 else None
+    case = jnp.sum((depth > jnp.array(cases, jnp.int32)).astype(jnp.int32))
+    chip_load = jnp.sum(
+        (of_chip[None, :] == jnp.arange(chips, dtype=jnp.int32)[:, None]).astype(jnp.int32), axis=1
+    )
+    load = jnp.max(chip_load)
+    width_case = jnp.sum((load > 2 * jnp.array(widths, jnp.int32)).astype(jnp.int32))
+    wide = jnp.array(widths, jnp.int32)[width_case]
     owner_first = me_work // per_row * ncols
     row_chip = lax.dynamic_slice_in_dim(of_chip, owner_first, ncols)
     row_rank = lax.dynamic_slice_in_dim(pair_rank, owner_first, ncols)
@@ -394,13 +570,34 @@
     back_slot = jnp.sum(jnp.where(returns, slot_rank, 0), axis=2)
     back_own = jnp.sum((returns & (assignment == me_work)).astype(jnp.int32), axis=2)
 
-    def by_depth(make, *args):
-        if len(cases) == 1:
-            return make(0, *args)
-        return lax.switch(case, [functools.partial(make, n) for n in range(len(cases))], *args)
+    def choose(index, makers, *args):
+        if len(makers) == 1:
+            return makers[0](*args)
+        return lax.switch(index, makers, *args)
+
+    sib_work = chip * 2 + 1 - core
+    sib_count = jnp.sum((assignment == sib_work).astype(jnp.int32))
+    kept = wide - jnp.maximum(sib_count - wide, 0)
+    wires = jnp.arange(slots, dtype=jnp.int32)
+    lent = (wires >= kept) & (wires < wide)
+    lent_slot = jnp.clip(wide + wires - kept, 0, slots - 1)
+    wire_slot = jnp.where(lent, sib_work * slots + lent_slot, me_work * slots + wires)
+    wire_block = jnp.take(block_ids, wire_slot)
+    wire_live = (jnp.take(filled, wire_slot) & (wires < wide)).astype(jnp.int32)
+    swap = [(w, w + 1 - 2 * (w % 2)) for w in range(workers)]
+    root = left_root
+    if len(widths) > 1:
+        low = widths[0]
+        sib_root = lax.ppermute(left_root[low:], "fsdp", swap)
+        root = wire_slots(
+            left_root,
+            sib_root,
+            jnp.where(lent, 0, wires),
+            jnp.where(lent, lent_slot - low, 0),
+            lent.astype(jnp.int32),
+        )
 
     summed = lax.psum_scatter(grad_parts[0], "replica", scatter_dimension=2, tiled=True)
-    left_wide = lax.all_gather(left_root, "replica", axis=0)
 
     my_blocks = lax.dynamic_slice_in_dim(block_ids, me_work * slots, slots)
     my_filled = lax.dynamic_slice_in_dim(filled, me_work * slots, slots)
@@ -427,14 +624,32 @@
     col_mask = global_rows[None, :] < col_widths[:, None]
     masked = jnp.where(col_mask[None], summed, jnp.zeros((), jnp.bfloat16))
 
-    def send_in(n, by_block, col):
-        outgoing = fill_outgoing(by_block, col, chips, cases[n])
-        return exchange(outgoing, most, True, 2 * n)
-
-    got = by_depth(send_in, jnp.transpose(masked, (1, 0, 2)), send_col)
-    my_rank = jnp.take(pair_rank, my_blocks)
-    g_cols, g_sq = pick_blocks(got, my_row, my_rank, my_filled.astype(jnp.int32), block_size)
-    g_all = lax.all_gather(g_cols, "replica", axis=0)
+    def send_in(n, by_block, col, root):
+        k, w = cases[n // len(widths)], widths[n % len(widths)]
+        return bring_in(fill_outgoing(by_block, col, chips, k), root, w, most, n)
+
+    pairs = len(cases) * len(widths)
+    got, left_wide = choose(
+        case * len(widths) + width_case,
+        [functools.partial(send_in, n) for n in range(pairs)],
+        jnp.transpose(masked, (1, 0, 2)),
+        send_col,
+        root,
+    )
+    my_live = my_filled.astype(jnp.int32)
+    g_cols, g_sq = pick_blocks(
+        got,
+        (wire_block // ncols, jnp.take(pair_rank, wire_block), wire_live),
+        (my_row, jnp.take(pair_rank, my_blocks), my_live),
+        block_size,
+    )
+
+    def spread_slots(n, shard):
+        return gather_slots(shard, widths[n], pairs + n)
+
+    g_all = choose(
+        width_case, [functools.partial(spread_slots, n) for n in range(len(widths))], g_cols
+    )
     left_trace, right_trace, grad_square = lax.psum(
         (left_part, right_part, jnp.sum(g_sq, axis=(1, 2))), "replica"
     )
@@ -444,23 +659,33 @@
         * (DECAY * right_trace + (1.0 - DECAY) * grad_square)
         / my_width.astype(jnp.float32)
     )
-    ints = jnp.stack([me_rep.astype(jnp.int32), my_count])
+    ints = jnp.stack([me_rep.astype(jnp.int32), my_count, wide])
     left_new, right_new, precond, p_sq = step_slots(
         ints, left_scale, right_scale, my_width, g_all, left_wide, right_root, left_stat, right_stat
     )
     split = precond.reshape(slots, hosts, 2, rows_dev, quarter)
-    swap = [(w, w + 1 - 2 * (w % 2)) for w in range(workers)]
     crossing = lax.dynamic_index_in_dim(split, 1 - core, 2, keepdims=False)
     sibling = lax.ppermute(crossing, "fsdp", swap)
 
     def send_back(n, mine, other, slot, own, core):
         outgoing = load_outgoing(mine, other, slot, own, core, chips, cases[n])
-        return exchange(outgoing, most, False, 2 * n + 1)
-
-    back = by_depth(send_back, split, sibling, back_slot, back_own, core[None])
-    precond_square = lax.psum(jnp.sum(p_sq, axis=(1, 2)), "replica")
-    graft_scale = jnp.sqrt(grad_square / (precond_square + EPSILON))
-    every_scale = lax.all_gather(graft_scale, "fsdp", axis=0, tiled=True)
+        return send_home(outgoing, most, pairs + len(widths) + n)
+
+    back = choose(
+        case,
+        [functools.partial(send_back, n) for n in range(len(cases))],
+        split,
+        sibling,
+        back_slot,
+        back_own,
+        core[None],
+    )
+    squares = jnp.stack([grad_square / REPLICAS, jnp.sum(p_sq, axis=(1, 2))])
+    placed = lax.dynamic_update_slice(
+        jnp.zeros((2, workers * slots), jnp.float32), squares, (0, me_work * slots)
+    )
+    placed = lax.psum(placed, ("replica", "fsdp"))
+    every_scale = jnp.sqrt(placed[0] / (placed[1] + EPSILON))
     owner_worker = lax.dynamic_slice_in_dim(assignment, owner_first, ncols)
     owner_slot = lax.dynamic_slice_in_dim(slot_rank, owner_first, ncols)
     my_scale = jnp.take(every_scale, owner_worker * slots + owner_slot)

time: 854 us -> 837 us (0.980)
  waiting for transfers between devices: 376 us -> 81.9 us
  Pallas kernels: 421 us -> 639 us
  blocking collectives: 28.1 us -> 46.6 us
  other arithmetic: 14.1 us -> 26.6 us
  starting transfers between devices: 0.12 us -> 10 us
    all_gather x2 -> x0, waiting for transfers between devices: 256 us -> none  [the longest x1 230 us: on_device(): g_all = lax.all_gather(g_cols, 'replica', axis=0)]
    pallas_call x2 -> x4, Pallas kernels: 325 us -> 547 us  [the longest x3 536 us: call(): pl.pallas_call(body, out_shape=[jax.ShapeDtypeStruct(shape, jnp.bfloat16)...]
    reduce_scatter x1, waiting for transfers between devices: 119 us -> 81.2 us  [on_device(): lax.psum_scatter(grad_parts[0], 'replica', scatter_dimension=2, tiled=True)]
    psum x1, blocking collectives: 8.96 us -> 37.6 us  [on_device(): placed = lax.psum(placed, ('replica', 'fsdp'))]
    pallas_call x1, Pallas kernels: 49.5 us -> 37.8 us  [step_slots(): pl.pallas_call(step_body, grid_spec=pltpu.PrefetchScalarGridSpec(num_scal...]
    unnamed x1 -> x0, blocking collectives: 10 us -> none
    ppermute x1, starting transfers between devices: 0.01 us -> 9.98 us  [on_device(): sibling = lax.ppermute(crossing, 'fsdp', swap)]
  transfers between devices with their start and end apart: 4 -> 3, of which waited for: 3 -> 1; matrix products, arithmetic and copies ran while one was open for 2% -> 4% of each run, Pallas kernels for 22% -> 1%
where the time goes in v3:
time: 837 us; the launch traced here: 839 us
  Pallas kernels  639 us (76%)
  waiting for transfers between devices  81.9 us (10%)
  blocking collectives  46.6 us (6%)
  other arithmetic  26.6 us (3%)
  between operations  21.1 us (3%)
  local copies, waits for them, and re-layouts  13.7 us (2%)
  starting transfers between devices  10 us (1%)
    pallas_call x3, Pallas kernels, call(): pl.pallas_call(body, out_shape=[jax.ShapeDtypeStruct(shape, jnp.bfloat16)...  536 us
    reduce_scatter x1, waiting for transfers between devices, on_device(): lax.psum_scatter(grad_parts[0], 'replica', scatter_dimension=2, tiled=True)  81.2 us
    pallas_call x1, Pallas kernels, step_slots(): pl.pallas_call(step_body, grid_spec=pltpu.PrefetchScalarGridSpec(num_scal...  37.8 us
    psum x1, blocking collectives, on_device(): placed = lax.psum(placed, ('replica', 'fsdp'))  37.6 us
    pallas_call x1, Pallas kernels, load_outgoing(): pl.pallas_call(load_body, grid_spec=pltpu.PrefetchScalarGridSpec(num_scal...  18.4 us
    pallas_call x1, Pallas kernels, fill_outgoing(): pl.pallas_call(fill_body, grid_spec=pltpu.PrefetchScalarGridSpec(num_scal...  18.1 us
  transfers between devices with their start and end apart: 3, of which 1 were waited for; matrix products, arithmetic and copies ran while one was open for 4% of the time, Pallas kernels for 1%

profile of v3, /device:TPU:8, one launch (start us, length us, event | category | flops | bytes accessed | tf_op | source)
XLA Modules:
  0.0 839.0 jit_solution(14316781791278646803)
XLA Ops:
  7.2 0.0 reduce-scatter.2.cloned.1.call-start
  7.3 0.7 reduce-scatter.2.cloned.1.call-update
  8.0 3.0 slice.9
  11.0 0.6 broadcast_compare_fusion.2
  11.6 0.1 dynamic_slice.31.chip
  11.7 0.2 convert_reduce_fusion.3
  11.9 0.1 dynamic_slice.32.rank
  11.9 0.6 reduce_max.19
  12.5 0.1 convert_reduce_fusion.4
  12.7 0.6 reduce_max.18
  13.3 1.3 fusion.5
  17.2 0.6 dynamic_slice.35
  17.8 0.2 convert_reduce_fusion.2
  18.0 0.5 copy-done.13
  18.5 0.6 fusion.6
  21.6 0.6 fusion.7
  23.4 0.7 fusion.8
  24.1 0.1 select_reduce_fusion.1
  24.2 0.7 gather_fusion.1
  24.8 0.7 gather_fusion
  25.5 0.7 and_select_fusion.3
  26.2 0.7 gather_fusion.4
  26.8 1.2 fusion.9
  28.0 1.2 and_convert_fusion
  29.2 0.5 compare_select_fusion.1
  29.8 0.7 gather_fusion.3
  30.5 0.2 select_reduce_fusion.3
  30.6 1.3 fusion.10
  31.9 1.9 pad_add_fusion.ints
  33.9 0.3 select_reduce_fusion
  34.2 4.6 multiply_reduce_fusion
  38.8 0.7 select_reduce_fusion.2
  39.5 1.3 add_select_fusion
  40.8 0.6 and_select_fusion.2.rank
  41.3 0.1 broadcast_compare_fusion
  41.4 10.5 %wire_slots.1 = bf16[12,1024,256]{2,1,0:T(8,128)(2,1)} custom-call(s32[12]{0:T(128)} %get-tuple-element.453.own_at, s32[12]{0:T(128)} %get-tuple-element.452.sib_at, s32[12]{0:T(128)} %get-tuple-element.436.use_sib, bf16[12,1024,256]{2,1,0:T(8,128)(2,1)} %own_ref.1, bf16[4,1024,256]{2,1,0:T(8,128)(2,1)} %collective-permute-done.sib_ref), custom_call_target="tpu_custom_call" | custom-call | tf_op jit(solution)/shard_map/wire_slots/pallas_call | solution.py:350
  51.9 81.2 %reduce-scatter.2.cloned.1.call-done = bf16[512,12,256]{2,0,1:T(8,128)(2,1)} async-done(((bf16[512,12,1024]{2,0,1:T(8,128)(2,1)}), bf16[512,12,256]{2,0,1:T(8,128)(2,1)}) %reduce-scatter.2.cloned.1.call-update) | async-done | bytes 3145744 | tf_op jit(solution)/shard_map/reduce_scatter | solution.py:600
  133.1 3.8 select_bitcast_fusion
  136.9 213.8 %conditional.3 = ((bf16[2,4,12,512,256]{4,3,2,1,0:T(8,128)(2,1)}, bf16[4,12,1024,256]{3,2,1,0:T(8,128)(2,1)})) conditional(s32[]{:T(128)} %clamp.19, (s32[4,12]{0,1:T(8,128)S(1)}, bf16[12,512,256]{2,1,0:T(8,128)(2,1)}, bf16[12,1024,256]{2,1,0:T(8,128)(2,1)}) %tuple.96, (s32[4,12]{0,1:T(8,128)S(1)}, ...), branch_computations={%region_12.14_spmd, %region_13.15_spmd, %region_14.16_spmd, %regio... | conditional | bytes 421528000 | solution.py:576
  136.9 0.7 copy.36.col
  137.6 18.1 %fill_outgoing.33.src = bf16[4,8,512,256]{3,2,1,0:T(8,128)(2,1)} custom-call(s32[4,12]{1,0:T(4,128)} %copy.36.col, bf16[12,512,256]{2,1,0:T(8,128)(2,1)} %get-tuple-element.226.in_ref), custom_call_target="tpu_custom_call" | custom-call | tf_op jit(solution)/shard_map/cond/branch_13_fun/fill_outgoing/pallas_call | solution.py:96
  155.6 194.8 %bring_in.33 = (bf16[2,4,12,512,256]{4,3,2,1,0:T(8,128)(2,1)}, bf16[4,12,1024,256]{3,2,1,0:T(8,128)(2,1)}) custom-call(bf16[4,8,512,256]{3,2,1,0:T(8,128)(2,1)} %fill_outgoing.33.src, bf16[12,1024,256]{2,1,0:T(8,128)(2,1)S(1)} %bitcast.26), custom_call_target="tpu_custom_call" | custom-call | bytes 268435456 | tf_op jit(solution)/shard_map/cond/branch_13_fun/bring_in/pallas_call | solution.py:268
  350.7 9.1 %pick_blocks.1 = (bf16[12,1024,256]{2,1,0:T(8,128)(2,1)S(1)}, f32[12,1,256]{2,1,0:T(1,128)}) custom-call(s32[12]{0:T(128)} %get-tuple-element.443.row, s32[12]{0:T(128)} %and_select_fusion.2.rank, s32[12]{0:T(128)} %get-tuple-element.438.live, s32[12]{0:T(128)} %get-tuple-element.450.own_row, s32[12]{0:T(128)} %get-tuple-element.456.own_rank, ...), custom_call_target="tpu_custom_call" | custom-call | tf_op jit(solution)/shard_map/pick_blocks/pallas_call | solution.py:65
  359.8 159.5 %conditional.4 = (bf16[4,12,1024,256]{3,2,1,0:T(8,128)(2,1)}) conditional(s32[]{:T(128)} %clamp.20, bf16[12,1024,256]{2,1,0:T(8,128)(2,1)S(1)} %get-tuple-element.284, bf16[12,1024,256]{2,1,0:T(8,128)(2,1)S(1)} %get-tuple-element.284, bf16[12,1024,256]{2,1,0:T(8,128)(2,1)S(1)} %get-tuple-element.284, ...), branch_computations={%region_41.43_spmd, %region_42.44_spmd, %region_43.45_spmd, %regio... | conditional | bytes 50331656 | solution.py:576
  359.8 159.5 %gather_slots.5 = bf16[4,12,1024,256]{3,2,1,0:T(8,128)(2,1)} custom-call(bf16[12,1024,256]{2,1,0:T(8,128)(2,1)S(1)} %src.1), custom_call_target="tpu_custom_call" | custom-call | bytes 50331648 | tf_op jit(solution)/shard_map/cond/branch_1_fun/gather_slots/pallas_call | solution.py:268
  519.3 0.2 reduce_sum.175
  519.5 8.9 %all-reduce = (f32[12]{0:T(128)S(1)}, f32[12]{0:T(128)S(1)}, f32[12]{0:T(128)S(1)}) all-reduce(f32[12]{0:T(128)S(1)} %copy-done.20, f32[12]{0:T(128)S(1)} %reduce_sum.175, f32[12]{0:T(128)S(1)} %copy-done.21), channel_id=1, replica_groups=mesh['replica'=4,'fsdp'=8] {'replica'}, use_global_device_ids=true, to_apply=%region_36.38 | all-reduce | flops 36 | bytes 288 | tf_op jit(solution)/shard_map/psum | solution.py:653
  528.4 0.5 multiply_bitcast_fusion
  529.0 37.8 %step_slots.1 = (f32[12,256,1024]{2,1,0:T(8,128)}, f32[12,256,1024]{2,1,0:T(8,128)}, bf16[12,1024,256]{2,1,0:T(8,128)(2,1)}, f32[12,1,256]{2,1,0:T(1,128)}) custom-call(s32[3]{0:T(128)} %pad_add_fusion.ints, f32[12]{0:T(128)} %get-tuple-element.447.lscale, f32[12]{0:T(128)} %get-tuple-element.446.rscale, s32[12]{0:T(128)} %copy-done.11, ...), custom_call_target="tpu_custom_call" | custom-call | tf_op jit(solution)/shard_map/step_slots/pallas_call | solution.py:442
  566.8 3.8 dynamic-slice_bitcast_fusion
  570.6 10.0 %collective-permute-start.1 = (bf16[12,1,512,256]{3,2,1,0:T(8,128)(2,1)}, bf16[12,1,512,256]{3,2,1,0:T(8,128)(2,1)S(1)}, u32[]{:S(2)}, u32[]{:S(2)}) collective-permute-start(bf16[12,1,512,256]{3,2,1,0:T(8,128)(2,1)} %dynamic-slice_bitcast_fusion), channel_id=1, source_target_pairs={{0,1},{1,0},{2,3},{3,2},{4,5},{5,4},{6,7},{7,6},{8,9},{9,8},{10,11... | collective-permute-start | bytes 9437192 | tf_op jit(solution)/shard_map/ppermute | solution.py:668
  581.1 0.1 compare_select_fusion.4
  581.3 0.5 convert_reduce_fusion
  581.8 0.9 reduce_sum.181
  582.7 0.3 dynamic_update_slice.3
  582.9 37.6 %psum.31 = f32[2,96]{1,0:T(2,128)S(1)} all-reduce(f32[2,96]{1,0:T(2,128)S(1)} %dynamic_update_slice.3), channel_id=1, replica_groups=mesh['replica'=4,'fsdp'=8] {'replica','fsdp'}, use_global_device_ids=true, to_apply=%region_46.48 | all-reduce | flops 192 | bytes 1536 | tf_op jit(solution)/shard_map/psum | solution.py:687
  620.6 0.7 gather_fusion.2
  621.2 0.5 and_select_fusion.7.scale
  621.8 201.6 %conditional.5 = (bf16[4,12,512,256]{3,2,1,0:T(8,128)(2,1)}) conditional(s32[]{:T(128)} %clamp.21, (s32[4,12]{0,1:T(8,128)S(1)}, s32[4,12]{0,1:T(8,128)S(1)}, s32[1]{0:T(128)}, bf16[12,1,2,512,256]{4,3,2,0,1:T(8,128)(2,1)}, bf16[12,1,512,256]{3,2,1,0:T(8,128)(2,1)S(1)}) %tuple.202, (s32[4,12]{0,1:T(8,128)S(1)}, ...), branch_computations={%region_49.51_spmd, %region_50.52_spmd, %region_51.53_spmd, %regio... | conditional | bytes 402653952 | solution.py:576
  621.8 0.7 copy.52.slot
  622.4 0.7 copy.53.own
  623.1 18.4 %load_outgoing.8.src = bf16[4,8,512,256]{3,2,1,0:T(8,128)(2,1)} custom-call(s32[4,12]{1,0:T(4,128)} %copy.52.slot, s32[4,12]{1,0:T(4,128)} %copy.53.own, s32[1]{0:T(128)} %get-tuple-element.263.core, bf16[12,1,2,512,256]{4,3,2,1,0:T(8,128)(2,1)} %bitcast.48, bf16[12,1,512,256]{3,2,1,0:T(8,128)(2,1)S(1)} %get-tuple-element.265.sib_ref), custom_call_target="tpu_custom_call" | custom-call | tf_op jit(solution)/shard_map/cond/branch_3_fun/load_outgoing/pallas_call | solution.py:480
  641.5 181.8 %send_home.8 = bf16[4,12,512,256]{3,2,1,0:T(8,128)(2,1)} custom-call(bf16[4,8,512,256]{3,2,1,0:T(8,128)(2,1)} %load_outgoing.8.src), custom_call_target="tpu_custom_call" | custom-call | bytes 268435456 | tf_op jit(solution)/shard_map/cond/branch_3_fun/send_home/pallas_call | solution.py:268
  823.4 8.7 %assemble.1 = bf16[12,512,256]{2,1,0:T(8,128)(2,1)} custom-call(s32[12]{0:T(128)} %copy-done.19, s32[12]{0:T(128)} %copy-done.17, f32[12]{0:T(128)} %and_select_fusion.7.scale, bf16[4,12,512,256]{3,2,1,0:T(8,128)(2,1)} %get-tuple-element.499.in_ref), custom_call_target="tpu_custom_call" | custom-call | tf_op jit(solution)/shard_map/assemble/pallas_call | solution.py:510
  (61 shorter events, 0.2 us)
Async XLA Ops:
  7.2 6.1 copy-start.26
  7.2 10.0 %copy-start.25 = (s32[4]{0:T(128)S(1)}, s32[4]{0:T(128)}, u32[]{:S(2)}) copy-start(s32[4]{0:T(128)} %constant.185.clone) | copy-start | bytes 52
  7.2 14.4 %copy-start.24 = (s32[5]{0:T(128)S(1)}, s32[5]{0:T(128)}, u32[]{:S(2)}) copy-start(s32[5]{0:T(128)} %constant.184.clone) | copy-start | bytes 64
  7.2 3.8 copy-start.15
  7.2 23.2 %copy-start.23 = (s32[12]{0:T(128)S(1)}, s32[12]{0:T(128)}, u32[]{:S(2)}) copy-start(s32[12]{0:T(128)} %param.42) | copy-start | bytes 148
  7.2 125.9 %reduce-scatter.2.cloned.1.call-start = ((), (), s32[]{:S(2)}) async-start(), calls=%async_computation.1 | async-start | bytes 15728640 | tf_op jit(solution)/shard_map/reduce_scatter | solution.py:600
  11.0 30.4 %collective-permute-start = (bf16[4,1024,256]{2,1,0:T(8,128)(2,1)}, bf16[4,1024,256]{2,1,0:T(8,128)(2,1)}, u32[]{:S(2)}, u32[]{:S(2)}) collective-permute-start(bf16[4,1024,256]{2,1,0:T(8,128)(2,1)} %slice.9), channel_id=1, source_target_pairs={{0,1},{1,0},{2,3},{3,2},{4,5},{5,4},{6,7},{7,6},{8,9},{9,8},{10,11... | collective-permute-start | bytes 6291464 | tf_op jit(solution)/shard_map/ppermute | solution.py:591
  11.7 22.2 %copy-start.19 = (s32[12]{0:T(128)}, s32[12]{0:T(128)S(1)}, u32[]{:S(2)}) copy-start(s32[12]{0:T(128)S(1)} %dynamic_slice.31.chip) | copy-start | bytes 148
  11.9 125.0 %copy-start.8 = (s32[48]{0:T(128)}, s32[48]{0:T(128)S(1)}, u32[]{:S(2)}) copy-start(s32[48]{0:T(128)S(1)} %convert_reduce_fusion.3) | copy-start | bytes 580
  11.9 21.9 %copy-start.17 = (s32[12]{0:T(128)}, s32[12]{0:T(128)S(1)}, u32[]{:S(2)}) copy-start(s32[12]{0:T(128)S(1)} %dynamic_slice.32.rank) | copy-start | bytes 148
  18.0 0.5 copy-start.13
  31.9 104.9 %copy-start.11 = (s32[12]{0:T(128)}, s32[12]{0:T(128)S(1)}, u32[]{:S(2)}) copy-start(s32[12]{0:T(128)S(1)} %get-tuple-element.448.width) | copy-start | bytes 148
  136.9 18.8 %slice-start.2 = ((s8[6291456]{0:T(1024)(128)(4,1)}), s8[2097152]{0:T(1024)(128)(4,1)S(1)}, s32[]{:S(2)}) async-start(s8[6291456]{0:T(1024)(128)(4,1)} %bitcast.25), calls=%async_computation.4 | async-start | bytes 4194304 | tf_op jit(solution)/shard_map/cond
  137.6 18.1 %slice-start.3 = ((s8[6291456]{0:T(1024)(128)(4,1)}), s8[4194304]{0:T(1024)(128)(4,1)S(1)}, s32[]{:S(2)}) async-start(s8[6291456]{0:T(1024)(128)(4,1)} %bitcast.25), calls=%async_computation.5 | async-start | bytes 8388608 | tf_op jit(solution)/shard_map/cond
  359.8 159.5 %copy-start.10 = (f32[12,1,256]{2,1,0:T(1,128)S(1)}, f32[12,1,256]{2,1,0:T(1,128)}, u32[]{:S(2)}) copy-start(f32[12,1,256]{2,1,0:T(1,128)} %get-tuple-element.283) | copy-start | bytes 36868
  359.8 159.7 %copy-start.20 = (f32[12]{0:T(128)S(1)}, f32[12]{0:T(128)}, u32[]{:S(2)}) copy-start(f32[12]{0:T(128)} %get-tuple-element.426) | copy-start | bytes 148
  359.8 159.7 %copy-start.21 = (f32[12]{0:T(128)S(1)}, f32[12]{0:T(128)}, u32[]{:S(2)}) copy-start(f32[12]{0:T(128)} %select_reduce_fusion.2) | copy-start | bytes 148
  359.8 168.7 %copy-start.12 = (s32[12]{0:T(128)S(1)}, s32[12]{0:T(128)}, u32[]{:S(2)}) copy-start(s32[12]{0:T(128)} %copy-done.11) | copy-start | bytes 148
  529.0 52.2 %copy-start.14 = (s32[48]{0:T(128)S(1)}, s32[48]{0:T(128)}, u32[]{:S(2)}) copy-start(s32[48]{0:T(128)} %copy-done.13) | copy-start | bytes 580
  529.0 52.2 %copy-start.16 = (s32[48]{0:T(128)S(1)}, s32[48]{0:T(128)}, u32[]{:S(2)}) copy-start(s32[48]{0:T(128)} %param.43) | copy-start | bytes 580
  529.0 52.3 %copy-start.22 = (pred[48]{0:T(512)(128)(4,1)S(1)}, pred[48]{0:T(512)(128)(4,1)}, u32[]{:S(2)}) copy-start(pred[48]{0:T(512)(128)(4,1)} %get-tuple-element.434) | copy-start | bytes 148
  529.0 52.3 %copy-start.9 = (s32[48]{0:T(128)S(1)}, s32[48]{0:T(128)}, u32[]{:S(2)}) copy-start(s32[48]{0:T(128)} %copy-done.8) | copy-start | bytes 580
  529.0 52.3 %copy-start.18 = (pred[48]{0:T(512)(128)(4,1)S(1)}, pred[48]{0:T(512)(128)(4,1)}, u32[]{:S(2)}) copy-start(pred[48]{0:T(512)(128)(4,1)} %get-tuple-element.444) | copy-start | bytes 148
  570.6 51.2 %collective-permute-start.1 = (bf16[12,1,512,256]{3,2,1,0:T(8,128)(2,1)}, bf16[12,1,512,256]{3,2,1,0:T(8,128)(2,1)S(1)}, u32[]{:S(2)}, u32[]{:S(2)}) collective-permute-start(bf16[12,1,512,256]{3,2,1,0:T(8,128)(2,1)} %dynamic-slice_bitcast_fusion), channel_id=1, source_target_pairs={{0,1},{1,0},{2,3},{3,2},{4,5},{5,4},{6,7},{7,6},{8,9},{9,8},{10,11... | collective-permute-start | bytes 9437192 | tf_op jit(solution)/shard_map/ppermute | solution.py:668
Sparse Core Ops, SparseCore 0:
  11.2 121.8 reduce-scatter.1
